TPU v7x, 128 devices: a whole 4x4x4 slice. The times are simulated.
128 devices in a mesh: train: 16 (over y, z), val: 8 (over x, core).
Axes of the slice: x: 4, y: 4, z: 4, core: 2. Of those that a mesh axis runs over, the one named last changes fastest.
Arguments:
- train_embed: bfloat16 [49152, 2048], P('train'), may hold values from -6 to 6
- val_embed: bfloat16 [8192, 2048], P('val', 'train'), may hold values from -6 to 6
- train_labels: int32 [49152], P('train'), may hold values from 0 to 9
- val_labels: int32 [8192], P('val'), may hold values from 0 to 9
- label_cost: float32 [10, 10], replicated, may hold values from 0.05 to 0.4
Outputs:
- train_potential: float32 [49152], P('train')
- val_potential: float32 [8192], P('val')
All inputs are finite; a program needn't handle non-finite values.
Results may differ from a plain program's by a relative error of at most 0.0003.
Values may be sent and summed in bfloat16 or wider, within the bound.
No kernel may reach another device: no remote copies, remote signals or barrier semaphores. Data moves between devices by JAX's collectives and lax.ppermute only.
A program may use at most 128 MiB of HBM per device.

v0:
```python
import math

import jax
import jax.numpy as jnp
from jax import lax
from jax.experimental import pallas as pl
from jax.experimental.pallas import tpu as pltpu
from jax.sharding import PartitionSpec as P

EPS = 0.01
LOG2E = math.log2(math.e)
KAPPA = LOG2E / EPS
VMEM = pl.BlockSpec(memory_space=pltpu.VMEM)
HBM = pl.BlockSpec(memory_space=pltpu.HBM)
LAST = (((1,), (1,)), ((), ()))
SPLITS = 16
SMALL = 10
SIDE = 4


def params(mib):
    return pltpu.CompilerParams(vmem_limit_bytes=mib << 20)


def in_vmem(x):
    return pltpu.with_memory_space_constraint(x, pltpu.VMEM)


def in_hbm(x):
    return pltpu.with_memory_space_constraint(x, pltpu.HBM)


def shape_of(shape, dtype=jnp.float32):
    return jax.ShapeDtypeStruct(shape, dtype)


def split_rows(x):
    n = x.shape[1]
    row = lax.broadcasted_iota(jnp.int32, (SPLITS, n), 0)
    hi = x.astype(jnp.bfloat16).astype(jnp.float32)
    mid = (x - hi).astype(jnp.bfloat16).astype(jnp.float32)
    low = x - hi - mid
    parts = jnp.where(row == 0, hi, jnp.where(row == 1, mid, jnp.where(row == 2, low, 0.0)))
    return parts.astype(jnp.bfloat16)


def logsum2(rows):
    peak = rows[0]
    for r in rows[1:]:
        peak = jnp.maximum(peak, r)
    total = jnp.exp2(rows[0] - peak)
    for r in rows[1:]:
        total = total + jnp.exp2(r - peak)
    return peak + jnp.log2(total)


def turn(block):
    r = lax.broadcasted_iota(jnp.int32, (128, 128), 0)
    c = lax.broadcasted_iota(jnp.int32, (128, 128), 1)
    return jnp.sum(jnp.where(r == c, block, 0.0), axis=0, keepdims=True)


def one_hot_rows(labels, slots):
    n = labels.shape[1]
    slot = lax.broadcasted_iota(jnp.int32, (128, n), 0)
    hot = ((slot % 16 == labels) & (slot < slots)).astype(jnp.float32)
    return jnp.transpose(hot).astype(jnp.bfloat16)


def prepare_kernel(
    features, tile, label_cost, train_labels, val_labels,
    source, train, train_hot, label_rows, labels, more_labels, costs, sems, label_sems,
):
    classes = label_cost.shape[0]
    label_copies = [
        pltpu.make_async_copy(train_labels, labels, label_sems.at[0]),
        pltpu.make_async_copy(val_labels, more_labels, label_sems.at[1]),
        pltpu.make_async_copy(label_cost, costs, label_sems.at[2]),
    ]
    spans = [pl.ds(k * tile, tile) for k in range(train.shape[0] // tile)]
    copies = [
        pltpu.make_async_copy(source.at[at], train.at[at], sems.at[k]) for k, at in enumerate(spans)
    ]
    for copy in label_copies + copies:
        copy.start()
    for copy in label_copies:
        copy.wait()
    table = jnp.pad(costs[...], ((0, 16 - classes), (0, 128 - classes))) * (-0.5 * features)
    hi = table.astype(jnp.bfloat16)
    rest = table - hi.astype(jnp.float32)
    mid = rest.astype(jnp.bfloat16)
    low = (rest - mid.astype(jnp.float32)).astype(jnp.bfloat16)
    table = jnp.concatenate([hi, mid, low, jnp.zeros((80, 128), jnp.bfloat16)], axis=0)
    out = lax.dot_general(
        one_hot_rows(more_labels[...], 16), table, LAST, preferred_element_type=jnp.float32
    )
    label_rows[...] = out.astype(jnp.bfloat16)
    train_hot[...] = one_hot_rows(labels[...], 48)
    for copy in copies:
        copy.wait()


def train_kernel(tile, log_cols, source, row_pot, r0, r1, r2, r3, out, squares, buf, sems):
    rows, features = source.shape
    count, depth = rows // tile, buf.shape[0]

    def fetch(k):
        at = pl.ds(k * tile, tile)
        slot = lax.rem(k, depth)
        return pltpu.make_async_copy(source.at[at], buf.at[slot], sems.at[slot])

    for k in range(depth - 1):
        fetch(k).start()
    @pl.loop(0, count)
    def _(k):
        @pl.when(k + depth - 1 < count)
        def _():
            fetch(k + depth - 1).start()

        fetch(k).wait()
        for r in range(0, tile, 64):
            total = jnp.zeros((64, 128), jnp.float32)
            for c in range(features // 128):
                piece = buf[lax.rem(k, depth), pl.ds(r, 64), pl.ds(c * 128, 128)].astype(jnp.float32)
                total = total + piece * piece
            squares[pl.ds(pl.multiple_of(k * tile + r, 64), 64), :] = total
    ones = jnp.ones((SPLITS, 128), jnp.bfloat16)
    rest, norm = squares[...], 0.0
    for _ in range(3):
        part = rest.astype(jnp.bfloat16)
        rest = rest - part.astype(jnp.float32)
        norm = norm + lax.dot_general(ones, part, LAST, preferred_element_type=jnp.float32)
    total = (r0[...] + r1[...]) + (r2[...] + r3[...])
    pot = (row_pot[...] + (log_cols - jnp.log2(total))) * (1.0 / KAPPA)
    out[...] = pot + norm[0:1, :] * (1.0 / features)


def part_kernel(plan, count, row, tile, alpha, *refs):
    vals, (train, *given), results = refs[:count], refs[count : count + 3], refs[count + 3 :]
    first, last = given[0].dtype == jnp.bfloat16, alpha is not None
    if first:
        label_rows, train_hot = given
    else:
        before, sq_before = given
    scores, out = results[:2]
    sq = results[2] if last else out
    rows = train.shape[0]
    half = scores.shape[0] // 2
    pieces = len(plan[0][2])
    to = pl.ds(row, half * pieces)
    t = lax.axis_index("train")
    y, z = t // SIDE, t % SIDE

    def piece(part, r, n):
        place, start = part
        return vals[place][pl.ds(start + r, n), :]

    for h in range(pieces):
        for r in range(0, half, 128):
            at = pl.ds(row + h * half + r, 128)
            total = jnp.zeros((128, 128), jnp.float32) if first else sq_before[at, :]
            for _, _, parts in plan:
                value = piece(parts[h], r, 128).astype(jnp.float32)
                total = total + value * value
            if last:
                total = jnp.sum(total, axis=1, keepdims=True) * 0.5
                sq[pl.ds(h * half + r, 128), :] = jnp.broadcast_to(total, (128, 128))
            else:
                sq[at, :] = total

    @pl.loop(0, rows // tile)
    def _(k):
        at = pl.ds(pl.multiple_of(k * tile, tile), tile)
        left, right = [], []
        for dy, dz, parts in plan:
            left.append(jnp.concatenate([piece(part, 0, half) for part in parts], axis=0))
            block = ((y + dy) % SIDE) * SIDE + (z + dz) % SIDE
            right.append(train[at, pl.ds(pl.multiple_of(block * 128, 128), 128)])
        if first:
            left.append(label_rows[to, :])
            right.append(train_hot[at, :])
        x = lax.dot_general(
            jnp.concatenate(left, axis=1),
            jnp.concatenate(right, axis=1),
            LAST,
            preferred_element_type=jnp.float32,
        )
        if not first:
            x = x + before[to, at]
        if last:
            x = (x - jnp.concatenate([sq[...]] * (tile // 128), axis=1)) * alpha
            peak = jnp.max(x, axis=0, keepdims=True)
            total = jnp.sum(jnp.exp2(x - peak), axis=0, keepdims=True)
            out[:, at] = peak + jnp.log2(total)
        scores[to, at] = x


def product_part(name, plan, row, tile, train, given, alpha=None):
    rows = train.shape[0]
    first, last = given[0].dtype == jnp.bfloat16, alpha is not None
    cols = given[0].shape[0]
    vals = []

    def place(array):
        for k, known in enumerate(vals):
            if known is array:
                return k
        vals.append(array)
        return len(vals) - 1

    plan = [(dy, dz, [(place(v), start) for v, start in parts]) for dy, dz, parts in plan]
    out = [pltpu.VMEM((cols, rows), jnp.float32)]
    out.append(shape_of((1, rows)) if last else shape_of((cols, 128)))
    given = given if first else [in_vmem(given[0]), given[1]]
    operands = [*vals, in_vmem(train), *given]
    depth = len(plan) * 128
    height = len(plan[0][2]) * cols // 2
    return pl.pallas_call(
        lambda *refs: part_kernel(plan, len(vals), row, tile, alpha, *refs),
        out_shape=tuple(out),
        in_specs=[VMEM] * len(operands),
        out_specs=(VMEM,) * len(out),
        scratch_shapes=[pltpu.VMEM((height, 128), jnp.float32)] if last else [],
        input_output_aliases={} if first else {len(operands) - 2: 0},
        compiler_params=params(SMALL),
        cost_estimate=pl.CostEstimate(
            flops=2 * height * rows * depth, bytes_accessed=0, transcendentals=0
        ),
        name=name,
    )(*operands)


def from_step(x, dy, dz):
    pairs = [
        (y * SIDE + z, ((y - dy) % SIDE) * SIDE + (z - dz) % SIDE)
        for y in range(SIDE)
        for z in range(SIDE)
    ]
    return lax.ppermute(x, "train", pairs)


def gather(x):
    h = x.shape[0] // 2
    low = lambda v, n: (v, n * h)
    cut = lambda v, n: v[n * h : (n + 1) * h]
    z1, z3 = from_step(x, 0, 1), from_step(x, 0, 3)
    y1, y3 = from_step(x, 1, 0), from_step(x, 3, 0)
    far = from_step(y1, 1, 2)
    both = lambda v: [low(v, 0), low(v, 1)]
    near = [(0, 0, both(x)), (0, 1, both(z1)), (0, 3, both(z3)), (1, 0, both(y1)), (3, 0, both(y3))]

    first = jnp.concatenate([cut(z1, 0), cut(z3, 0)], axis=0)
    second = jnp.concatenate([cut(y1, 1), cut(y3, 1)], axis=0)
    a1, a3 = from_step(first, 1, 0), from_step(first, 3, 0)
    b1, b3 = from_step(second, 0, 1), from_step(second, 0, 3)
    diagonal = [
        (dy, dz, [low(a, i), low(b, j)])
        for j, (dy, a) in enumerate(((1, a1), (3, a3)))
        for i, (dz, b) in enumerate(((1, b1), (3, b3)))
    ]
    diagonal.append((2, 2, both(far)))

    join = lambda *v: jnp.concatenate(v, axis=0)
    az = from_step(join(cut(z1, 0), cut(a1, 0), cut(a3, 0)), 0, 1)
    bz = from_step(join(cut(z3, 1), b3), 0, 3)
    by = from_step(join(cut(y1, 1), cut(b1, 0), cut(b3, 0)), 1, 0)
    ay = from_step(join(cut(y3, 0), a3), 3, 0)
    across = [(0, 2), (1, 2), (3, 2)]
    along = [(2, 0), (2, 1), (2, 3)]
    last_a = [(*d, [low(az, k)]) for k, d in enumerate(across)]
    last_a += [(*d, [low(ay, k)]) for k, d in enumerate(along)]
    last_b = [(*d, [low(bz, k)]) for k, d in enumerate(across)]
    last_b += [(*d, [low(by, k)]) for k, d in enumerate(along)]
    return near, diagonal, last_a, last_b


def kernel_kernel(log_cols, scores, l0, l1, l2, l3, kern, row_pot, peaks, col_log, peak_b, log_b):
    cols, rows = scores.shape
    pot = log_cols - logsum2([l0[...], l1[...], l2[...], l3[...]])
    row_pot[...] = pot
    block = 64

    @pl.loop(0, cols // block, unroll=4)
    def _(k):
        part = pl.ds(pl.multiple_of(k * block, block), block)
        peak = None
        for c in range(rows // 128):
            lane = pl.ds(c * 128, 128)
            x = scores[part, lane] + row_pot[:, lane]
            peak = x if peak is None else jnp.maximum(peak, x)
        peak = jnp.max(peak, axis=1, keepdims=True)
        peak = jnp.broadcast_to(peak, (block, 128))
        total = jnp.zeros((block, 128), jnp.float32)
        for c in range(rows // 128):
            lane = pl.ds(c * 128, 128)
            e = jnp.exp2((scores[part, lane] - peak) + row_pot[:, lane])
            total = total + e
            kern[part, lane] = e.astype(kern.dtype)
        total = jnp.sum(total, axis=1, keepdims=True)
        peak_b[part, :] = peak
        log_b[part, :] = peak + jnp.log2(total)

    for k in range(cols // 128):
        part = pl.ds(k * 128, 128)
        peaks[:, part] = turn(peak_b[part, :])
        col_log[:, part] = jnp.broadcast_to(turn(log_b[part, :]), (col_log.shape[0], 128))


def first_rows_kernel(total_rows, kern, peaks, col_logs, weights, first_log, sums):
    logs = col_logs[...]
    peak = jnp.max(logs, axis=0, keepdims=True)
    whole = peak + jnp.log2(jnp.sum(jnp.exp2(logs - peak), axis=0, keepdims=True))
    first_log[...] = whole
    v = jnp.exp2(peaks[...] - whole) * total_rows
    weights[...] = v
    out = jnp.dot(split_rows(v), kern[...], preferred_element_type=jnp.float32)
    sums[...] = jnp.sum(out, axis=0, keepdims=True)


def next_rows_kernel(total_rows, kern, weights, col_sums, sums):
    v = weights[...] * (total_rows / jnp.sum(col_sums[...], axis=0, keepdims=True))
    out = jnp.dot(split_rows(v), kern[...], preferred_element_type=jnp.float32)
    sums[...] = jnp.sum(out, axis=0, keepdims=True)


def cols_kernel(total_cols, kern, weights, r0, r1, r2, r3, sums):
    u = total_cols / ((r0[...] + r1[...]) + (r2[...] + r3[...]))
    out = lax.dot_general(split_rows(u), kern[...], LAST, preferred_element_type=jnp.float32)
    out = jnp.sum(out, axis=0, keepdims=True) * weights[...]
    sums[...] = jnp.broadcast_to(out, sums.shape)


def other_chips(x):
    n = lax.axis_size("val")
    return [
        lax.ppermute(x, "val", [(i, (i + 2 * k) % n) for i in range(n)]) for k in range(1, n // 2)
    ]


def other_core(x):
    return lax.ppermute(x, "val", [(i, i ^ 1) for i in range(lax.axis_size("val"))])


def spread(x):
    n = lax.axis_size("train")
    return lax.all_to_all(x.reshape(n, 1, -1), "train", 0, 0).reshape(n, -1)


def shards(train_embed, val_embed, train_labels, val_labels, label_cost):
    rows, features = train_embed.shape
    cols = val_embed.shape[0]
    groups = lax.axis_size("train")
    total_rows = float(rows * groups)
    total_cols = float(cols * lax.axis_size("val"))
    vec_r, vec_c = shape_of((1, rows)), shape_of((1, cols))

    near, diagonal, last_a, last_b = gather(val_embed)
    train, train_hot, label_rows = pl.pallas_call(
        lambda *refs: prepare_kernel(features, 512, *refs),
        out_shape=(
            pltpu.VMEM((rows, features), jnp.bfloat16),
            shape_of((rows, 128), jnp.bfloat16),
            shape_of((cols, 128), jnp.bfloat16),
        ),
        in_specs=[HBM] * 4,
        out_specs=(VMEM,) * 3,
        scratch_shapes=[
            pltpu.VMEM((1, rows), jnp.int32),
            pltpu.VMEM((1, cols), jnp.int32),
            pltpu.VMEM(label_cost.shape, jnp.float32),
            pltpu.SemaphoreType.DMA((rows // 512,)),
            pltpu.SemaphoreType.DMA((3,)),
        ],
        compiler_params=params(SMALL),
        name="prepare",
    )(
        in_hbm(label_cost),
        in_hbm(train_labels.reshape(1, rows)),
        in_hbm(val_labels.reshape(1, cols)),
        in_hbm(train_embed),
    )
    alpha = 2.0 * KAPPA / features
    given = product_part("product_near", near, 0, 1024, train, [label_rows, train_hot])
    scores, squares = product_part("product_diagonal", diagonal, 0, 1024, train, given)
    scores, log_a = product_part("product_a", last_a, 0, 1024, train, [scores, squares], alpha)
    scores, log_b = product_part(
        "product_b", last_b, cols // 2, 1024, train, [scores, squares], alpha
    )
    row_log = jnp.logaddexp2(log_a, log_b)

    both = jnp.logaddexp2(row_log, other_core(row_log))
    kern, row_pot, peaks, col_log = pl.pallas_call(
        lambda *refs: kernel_kernel(math.log2(total_cols), *refs),
        out_shape=(shape_of((cols, rows), jnp.bfloat16), vec_r, vec_c, shape_of((groups, cols))),
        in_specs=[VMEM] * 5,
        out_specs=(VMEM,) * 4,
        scratch_shapes=[pltpu.VMEM((cols, 128), jnp.float32)] * 2,
        compiler_params=params(SMALL),
        name="kernel_matrix",
    )(scores, both, *other_chips(both))

    weights, first_log, sums = pl.pallas_call(
        lambda *refs: first_rows_kernel(total_rows, *refs),
        out_shape=(vec_c, vec_c, vec_r),
        in_specs=[VMEM] * 3,
        out_specs=(VMEM,) * 3,
        compiler_params=params(SMALL),
        name="first_rows",
    )(kern, peaks, spread(col_log))

    for sweep in range(2):
        both = sums + other_core(sums)
        others = other_chips(both)
        col_sums = pl.pallas_call(
            lambda *refs: cols_kernel(total_cols, *refs),
            out_shape=shape_of((groups, cols)),
            in_specs=[VMEM] * 6,
            out_specs=VMEM,
            compiler_params=params(SMALL),
            name="columns",
        )(kern, weights, both, *others)
        col_sums = spread(col_sums)
        if sweep == 0:
            sums = pl.pallas_call(
                lambda *refs: next_rows_kernel(total_rows, *refs),
                out_shape=vec_r,
                in_specs=[VMEM] * 3,
                out_specs=VMEM,
                compiler_params=params(SMALL),
                name="rows",
            )(kern, weights, col_sums)

    train_potential = pl.pallas_call(
        lambda *refs: train_kernel(256, math.log2(total_cols), *refs),
        out_shape=vec_r,
        in_specs=[HBM] + [VMEM] * 5,
        out_specs=VMEM,
        scratch_shapes=[
            pltpu.VMEM((rows, 128), jnp.float32),
            pltpu.VMEM((7, 256, features), jnp.bfloat16),
            pltpu.SemaphoreType.DMA((7,)),
        ],
        compiler_params=params(14),
        name="train_potential",
    )(in_hbm(train_embed), row_pot, both, *others).reshape(rows)
    col_total = jnp.sum(col_sums, axis=0, keepdims=True)
    val_potential = ((2.0 * math.log2(total_rows) - first_log) - jnp.log2(col_total)) / KAPPA
    return train_potential, val_potential.reshape(cols)


def solution(mesh):
    return jax.shard_map(
        shards,
        mesh=mesh,
        in_specs=(P("train", None), P("val", "train"), P("train"), P("val"), P()),
        out_specs=(P("train"), P("val")),
        check_vma=False,
    )
```

profile of v0, /device:TPU:0, one launch (start us, length us, event | category | flops | bytes accessed | tf_op | source)
XLA Modules:
  0.0 122.5 jit_solution(10634485852283383575)
XLA Ops:
  0.6 3.2 %collective-permute-start.1 = (bf16[1024,128]{1,0:T(8,128)(2,1)}, bf16[1024,128]{1,0:T(8,128)(2,1)S(1)}, u32[]{:S(2)}, u32[]{:S(2)}) collective-permute-start(bf16[1024,128]{1,0:T(8,128)(2,1)} %refs_0_.4), channel_id=1, source_target_pairs={{0,96},{8,104},{16,112},{24,120},{32,0},{40,8},{48,16},{56,24},{64... | collective-permute-start | bytes 786440 | tf_op jit(solution)/shard_map/ppermute | solution.py:239
  3.8 1.9 %collective-permute-start = (bf16[1024,128]{1,0:T(8,128)(2,1)}, bf16[1024,128]{1,0:T(8,128)(2,1)S(1)}, u32[]{:S(2)}, u32[]{:S(2)}) collective-permute-start(bf16[1024,128]{1,0:T(8,128)(2,1)} %refs_0_.4), channel_id=1, source_target_pairs={{0,8},{8,16},{16,24},{24,0},{32,40},{40,48},{48,56},{56,32},{64,72... | collective-permute-start | bytes 786440 | tf_op jit(solution)/shard_map/ppermute | solution.py:239
  5.7 2.1 %collective-permute-start.7 = (bf16[1024,128]{1,0:T(8,128)(2,1)}, bf16[1024,128]{1,0:T(8,128)(2,1)S(1)}, u32[]{:S(2)}, u32[]{:S(2)}) collective-permute-start(bf16[1024,128]{1,0:T(8,128)(2,1)} %refs_0_.4), channel_id=1, source_target_pairs={{0,24},{8,0},{16,8},{24,16},{32,56},{40,32},{48,40},{56,48},{64,88... | collective-permute-start | bytes 786440 | tf_op jit(solution)/shard_map/ppermute | solution.py:239
  7.9 4.8 %prepare.1 = (bf16[3072,2048]{1,0:T(8,128)(2,1)S(1)}, bf16[3072,128]{1,0:T(8,128)(2,1)S(1)}, bf16[1024,128]{1,0:T(8,128)(2,1)S(1)}) custom-call(f32[10,10]{1,0:T(8,128)} %refs_0_.3, s32[1,3072]{1,0:T(1,128)} %bitcast.20, s32[1,1024]{1,0:T(1,128)} %bitcast.22, bf16[3072,2048]{1,0:T(8,128)(2,1)} %refs_0_.5), custom_call_target="tpu_custom_call" | custom-call | tf_op jit(solution)/shard_map/prepare/pallas_call | solution.py:358
  13.0 2.0 %collective-permute-start.3 = (bf16[1024,128]{1,0:T(8,128)(2,1)S(1)}, bf16[1024,128]{1,0:T(8,128)(2,1)S(1)}, u32[]{:S(2)}, u32[]{:S(2)}) collective-permute-start(bf16[1024,128]{1,0:T(8,128)(2,1)S(1)} %pad_maximum_fusion.4), channel_id=1, source_target_pairs={{0,8},{8,16},{16,24},{24,0},{32,40},{40,48},{48,56},{56,32},{64,72... | collective-permute-start | bytes 786440 | tf_op jit(solution)/shard_map/ppermute | solution.py:239
  15.0 2.2 %collective-permute-start.5 = (bf16[1024,128]{1,0:T(8,128)(2,1)S(1)}, bf16[1024,128]{1,0:T(8,128)(2,1)S(1)}, u32[]{:S(2)}, u32[]{:S(2)}) collective-permute-start(bf16[1024,128]{1,0:T(8,128)(2,1)S(1)} %pad_maximum_fusion.4), channel_id=1, source_target_pairs={{0,24},{8,0},{16,8},{24,16},{32,56},{40,32},{48,40},{56,48},{64,88... | collective-permute-start | bytes 786440 | tf_op jit(solution)/shard_map/ppermute | solution.py:239
  17.4 3.2 %collective-permute-start.8 = (bf16[1024,128]{1,0:T(8,128)(2,1)S(1)}, bf16[1024,128]{1,0:T(8,128)(2,1)S(1)}, u32[]{:S(2)}, u32[]{:S(2)}) collective-permute-start(bf16[1024,128]{1,0:T(8,128)(2,1)S(1)} %pad_maximum_fusion.5), channel_id=1, source_target_pairs={{0,96},{8,104},{16,112},{24,120},{32,0},{40,8},{48,16},{56,24},{64... | collective-permute-start | bytes 786440 | tf_op jit(solution)/shard_map/ppermute | solution.py:239
  21.8 5.7 %product_near.1 = (f32[1024,3072]{1,0:T(8,128)S(1)}, f32[1024,128]{1,0:T(8,128)S(1)}) custom-call(bf16[1024,128]{1,0:T(8,128)(2,1)S(1)} %copy-done, bf16[1024,128]{1,0:T(8,128)(2,1)S(1)} %collective-permute-done.7.refs_1_, bf16[1024,128]{1,0:T(8,128)(2,1)S(1)} %collective-permute-done.refs_2_, bf16[1024,128]{1,0:T(8,128)(2,1)S(1)} %collective-permute-done.1.refs_3_, ...), custom_call_target="tpu_custom_call" | custom-call | flops 4026531840 | tf_op jit(solution)/shard_map/product_near/pallas_call | solution.py:218
  30.6 2.3 %collective-permute-start.6 = (bf16[1536,128]{1,0:T(8,128)(2,1)S(1)}, bf16[1536,128]{1,0:T(8,128)(2,1)S(1)}, u32[]{:S(2)}, u32[]{:S(2)}) collective-permute-start(bf16[1536,128]{1,0:T(8,128)(2,1)S(1)} %pad_maximum_fusion.1), channel_id=1, source_target_pairs={{0,96},{8,104},{16,112},{24,120},{32,0},{40,8},{48,16},{56,24},{64... | collective-permute-start | bytes 1179656 | tf_op jit(solution)/shard_map/ppermute | solution.py:239
  33.6 6.8 %product_diagonal.1 = (f32[1024,3072]{1,0:T(8,128)S(1)}, f32[1024,128]{1,0:T(8,128)S(1)}) custom-call(bf16[1024,128]{1,0:T(8,128)(2,1)S(1)} %collective-permute-done.8.refs_0_, bf16[1024,128]{1,0:T(8,128)(2,1)S(1)} %collective-permute-done.5.refs_1_, bf16[1024,128]{1,0:T(8,128)(2,1)S(1)} %collective-permute-done.3.refs_2_, ...), custom_call_target="tpu_custom_call", output_to_operand_aliasing={{0}: (6, {})} | custom-call | flops 4026531840 | tf_op jit(solution)/shard_map/product_diagonal/pallas_call | solution.py:218
  40.5 4.9 %product_a.1 = (f32[1024,3072]{1,0:T(8,128)S(1)}, f32[1,3072]{1,0:T(1,128)S(1)}) custom-call(bf16[1536,128]{1,0:T(8,128)(2,1)S(1)} %collective-permute-done.10.refs_0_, bf16[1536,128]{1,0:T(8,128)(2,1)S(1)} %collective-permute-done.11.refs_1_, bf16[3072,2048]{1,0:T(8,128)(2,1)S(1)} %get-tuple-element.20.refs_5_.refs_2_, ...), custom_call_target="tpu_custom_call", output_to_operand_aliasing={{0}: (3, {})} | custom-call | flops 2415919104 | tf_op jit(solution)/shard_map/product_a/pallas_call | solution.py:218
  45.4 4.9 %product_b.1 = (f32[1024,3072]{1,0:T(8,128)S(1)}, f32[1,3072]{1,0:T(1,128)S(1)}) custom-call(bf16[1536,128]{1,0:T(8,128)(2,1)S(1)} %collective-permute-done.4.refs_0_, bf16[1536,128]{1,0:T(8,128)(2,1)S(1)} %collective-permute-done.6.refs_1_, bf16[3072,2048]{1,0:T(8,128)(2,1)S(1)} %get-tuple-element.20.refs_5_.refs_2_, ...), custom_call_target="tpu_custom_call", output_to_operand_aliasing={{0}: (3, {})} | custom-call | flops 2415919104 | tf_op jit(solution)/shard_map/product_b/pallas_call | solution.py:218
  51.7 1.6 %collective-permute-start.14 = (f32[1,3072]{1,0:T(1,128)S(1)}, f32[1,3072]{1,0:T(1,128)S(1)}, u32[]{:S(2)}, u32[]{:S(2)}) collective-permute-start(f32[1,3072]{1,0:T(1,128)S(1)} %compare_select_fusion.refs_1_), channel_id=1, source_target_pairs={{0,2},{1,3},{2,4},{3,5},{4,6},{5,7},{6,0},{7,1},{8,10},{9,11},{10,... | collective-permute-start | bytes 36872 | tf_op jit(solution)/shard_map/ppermute | solution.py:336
  53.3 2.7 %collective-permute-start.15 = (f32[1,3072]{1,0:T(1,128)S(1)}, f32[1,3072]{1,0:T(1,128)S(1)}, u32[]{:S(2)}, u32[]{:S(2)}) collective-permute-start(f32[1,3072]{1,0:T(1,128)S(1)} %compare_select_fusion.refs_1_), channel_id=1, source_target_pairs={{0,4},{1,5},{2,6},{3,7},{4,0},{5,1},{6,2},{7,3},{8,12},{9,13},{10,... | collective-permute-start | bytes 36872 | tf_op jit(solution)/shard_map/ppermute | solution.py:336
  59.7 3.6 %kernel_matrix.1 = (bf16[1024,3072]{1,0:T(8,128)(2,1)S(1)}, f32[1,3072]{1,0:T(1,128)S(1)}, f32[1,1024]{1,0:T(1,128)S(1)}, f32[16,1024]{1,0:T(8,128)S(1)}) custom-call(f32[1024,3072]{1,0:T(8,128)S(1)} %get-tuple-element.28.refs_0_, f32[1,3072]{1,0:T(1,128)S(1)} %compare_select_fusion.refs_1_, f32[1,3072]{1,0:T(1,128)S(1)} %collective-permute-done.14.refs_2_, ...), custom_call_target="tpu_custom_call" | custom-call | tf_op jit(solution)/shard_map/kernel_matrix/pallas_call | solution.py:392
  63.4 13.1 %all_to_all.15 = f32[16,1,1024]{2,1,0:T(1,128)S(1)} all-to-all(f32[16,1,1024]{2,1,0:T(1,128)S(1)} %copy.10), channel_id=1, replica_groups=mesh['train'=16,'val'=8] {'train'}, dimensions={0} | all-to-all | bytes 131072 | tf_op jit(solution)/shard_map/all_to_all | solution.py:346
  79.1 3.8 %collective-permute-start.19 = (f32[1,3072]{1,0:T(1,128)S(1)}, f32[1,3072]{1,0:T(1,128)S(1)}, u32[]{:S(2)}, u32[]{:S(2)}) collective-permute-start(f32[1,3072]{1,0:T(1,128)S(1)} %add.22.refs_2_), channel_id=1, source_target_pairs={{0,4},{1,5},{2,6},{3,7},{4,0},{5,1},{6,2},{7,3},{8,12},{9,13},{10,... | collective-permute-start | bytes 36872 | tf_op jit(solution)/shard_map/ppermute | solution.py:336
  84.7 1.9 %collective-permute-done.20.refs_5_ = f32[1,3072]{1,0:T(1,128)S(1)} collective-permute-done((f32[1,3072]{1,0:T(1,128)S(1)}, f32[1,3072]{1,0:T(1,128)S(1)}, u32[]{:S(2)}, u32[]{:S(2)}) %collective-permute-start.20) | collective-permute-done | bytes 12320 | tf_op jit(solution)/shard_map/ppermute | solution.py:336
  86.6 1.7 %columns.2 = f32[16,1024]{1,0:T(8,128)S(1)} custom-call(bf16[1024,3072]{1,0:T(8,128)(2,1)S(1)} %get-tuple-element.32.refs_0_, f32[1,1024]{1,0:T(1,128)S(1)} %get-tuple-element.35.refs_1_, f32[1,3072]{1,0:T(1,128)S(1)} %add.22.refs_2_, f32[1,3072]{1,0:T(1,128)S(1)} %collective-permute-done.18.refs_3_, f32[1,3072]{1,0:T(1,128)S(1)} %collective-permute-done.19.refs_4_, ...), custom_call_target="tpu_custom_call" | custom-call | tf_op jit(solution)/shard_map/columns/pallas_call | solution.py:414
  88.5 10.9 %all_to_all.16 = f32[16,1,1024]{2,1,0:T(1,128)S(1)} all-to-all(f32[16,1,1024]{2,1,0:T(1,128)S(1)} %copy.11), channel_id=1, replica_groups=mesh['train'=16,'val'=8] {'train'}, dimensions={0} | all-to-all | bytes 131072 | tf_op jit(solution)/shard_map/all_to_all | solution.py:346
  101.9 2.7 %collective-permute-start.23 = (f32[1,3072]{1,0:T(1,128)S(1)}, f32[1,3072]{1,0:T(1,128)S(1)}, u32[]{:S(2)}, u32[]{:S(2)}) collective-permute-start(f32[1,3072]{1,0:T(1,128)S(1)} %add.23.refs_2_), channel_id=1, source_target_pairs={{0,4},{1,5},{2,6},{3,7},{4,0},{5,1},{6,2},{7,3},{8,12},{9,13},{10,... | collective-permute-start | bytes 36872 | tf_op jit(solution)/shard_map/ppermute | solution.py:336
  108.3 1.7 %columns.3 = f32[16,1024]{1,0:T(8,128)S(1)} custom-call(bf16[1024,3072]{1,0:T(8,128)(2,1)S(1)} %get-tuple-element.32.refs_0_, f32[1,1024]{1,0:T(1,128)S(1)} %get-tuple-element.35.refs_1_, f32[1,3072]{1,0:T(1,128)S(1)} %add.23.refs_2_, f32[1,3072]{1,0:T(1,128)S(1)} %collective-permute-done.22.refs_3_, f32[1,3072]{1,0:T(1,128)S(1)} %collective-permute-done.23.refs_4_, ...), custom_call_target="tpu_custom_call" | custom-call | tf_op jit(solution)/shard_map/columns/pallas_call | solution.py:414
  110.8 3.5 %all-to-all-start.2 = ((f32[16,1,1024]{2,1,0:T(1,128)}), f32[16,1,1024]{2,1,0:T(1,128)S(1)}, u32[]{:S(2)}, u32[]{:S(2)}) async-start(f32[16,1,1024]{2,1,0:T(1,128)} %copy.12), calls=%async_computation.2 | async-start | bytes 131072 | tf_op jit(solution)/shard_map/all_to_all | solution.py:346
  114.3 6.4 %train_potential.1 = f32[1,3072]{1,0:T(1,128)} custom-call(bf16[3072,2048]{1,0:T(8,128)(2,1)} %refs_0_.5, f32[1,3072]{1,0:T(1,128)S(1)} %get-tuple-element.31.refs_1_, f32[1,3072]{1,0:T(1,128)S(1)} %add.23.refs_2_, f32[1,3072]{1,0:T(1,128)S(1)} %collective-permute-done.22.refs_3_, f32[1,3072]{1,0:T(1,128)S(1)} %collective-permute-done.23.refs_4_, ...), custom_call_target="tpu_custom_call" | custom-call | tf_op jit(solution)/shard_map/train_potential/pallas_call | solution.py:433
  (69 shorter events, 23.9 us)
Async XLA Ops:
  0.6 12.0 %collective-permute-start.1 = (bf16[1024,128]{1,0:T(8,128)(2,1)}, bf16[1024,128]{1,0:T(8,128)(2,1)S(1)}, u32[]{:S(2)}, u32[]{:S(2)}) collective-permute-start(bf16[1024,128]{1,0:T(8,128)(2,1)} %refs_0_.4), channel_id=1, source_target_pairs={{0,96},{8,104},{16,112},{24,120},{32,0},{40,8},{48,16},{56,24},{64... | collective-permute-start | bytes 786440 | tf_op jit(solution)/shard_map/ppermute | solution.py:239
  3.8 9.2 %collective-permute-start.2 = (bf16[1024,128]{1,0:T(8,128)(2,1)}, bf16[1024,128]{1,0:T(8,128)(2,1)S(1)}, u32[]{:S(2)}, u32[]{:S(2)}) collective-permute-start(bf16[1024,128]{1,0:T(8,128)(2,1)} %refs_0_.4), channel_id=1, source_target_pairs={{0,32},{8,40},{16,48},{24,56},{32,64},{40,72},{48,80},{56,88},{64,... | collective-permute-start | bytes 786440 | tf_op jit(solution)/shard_map/ppermute | solution.py:239
  3.8 13.4 %collective-permute-start = (bf16[1024,128]{1,0:T(8,128)(2,1)}, bf16[1024,128]{1,0:T(8,128)(2,1)S(1)}, u32[]{:S(2)}, u32[]{:S(2)}) collective-permute-start(bf16[1024,128]{1,0:T(8,128)(2,1)} %refs_0_.4), channel_id=1, source_target_pairs={{0,8},{8,16},{16,24},{24,0},{32,40},{40,48},{48,56},{56,32},{64,72... | collective-permute-start | bytes 786440 | tf_op jit(solution)/shard_map/ppermute | solution.py:239
  5.7 11.5 %collective-permute-start.7 = (bf16[1024,128]{1,0:T(8,128)(2,1)}, bf16[1024,128]{1,0:T(8,128)(2,1)S(1)}, u32[]{:S(2)}, u32[]{:S(2)}) collective-permute-start(bf16[1024,128]{1,0:T(8,128)(2,1)} %refs_0_.4), channel_id=1, source_target_pairs={{0,24},{8,0},{16,8},{24,16},{32,56},{40,32},{48,40},{56,48},{64,88... | collective-permute-start | bytes 786440 | tf_op jit(solution)/shard_map/ppermute | solution.py:239
  13.0 17.5 %collective-permute-start.3 = (bf16[1024,128]{1,0:T(8,128)(2,1)S(1)}, bf16[1024,128]{1,0:T(8,128)(2,1)S(1)}, u32[]{:S(2)}, u32[]{:S(2)}) collective-permute-start(bf16[1024,128]{1,0:T(8,128)(2,1)S(1)} %pad_maximum_fusion.4), channel_id=1, source_target_pairs={{0,8},{8,16},{16,24},{24,0},{32,40},{40,48},{48,56},{56,32},{64,72... | collective-permute-start | bytes 786440 | tf_op jit(solution)/shard_map/ppermute | solution.py:239
  15.0 15.6 %collective-permute-start.5 = (bf16[1024,128]{1,0:T(8,128)(2,1)S(1)}, bf16[1024,128]{1,0:T(8,128)(2,1)S(1)}, u32[]{:S(2)}, u32[]{:S(2)}) collective-permute-start(bf16[1024,128]{1,0:T(8,128)(2,1)S(1)} %pad_maximum_fusion.4), channel_id=1, source_target_pairs={{0,24},{8,0},{16,8},{24,16},{32,56},{40,32},{48,40},{56,48},{64,88... | collective-permute-start | bytes 786440 | tf_op jit(solution)/shard_map/ppermute | solution.py:239
  17.3 10.2 %collective-permute-start.9 = (bf16[1024,128]{1,0:T(8,128)(2,1)S(1)}, bf16[1024,128]{1,0:T(8,128)(2,1)S(1)}, u32[]{:S(2)}, u32[]{:S(2)}) collective-permute-start(bf16[1024,128]{1,0:T(8,128)(2,1)S(1)} %pad_maximum_fusion.5), channel_id=1, source_target_pairs={{0,32},{8,40},{16,48},{24,56},{32,64},{40,72},{48,80},{56,88},{64,... | collective-permute-start | bytes 786440 | tf_op jit(solution)/shard_map/ppermute | solution.py:239
  17.4 10.2 %collective-permute-start.8 = (bf16[1024,128]{1,0:T(8,128)(2,1)S(1)}, bf16[1024,128]{1,0:T(8,128)(2,1)S(1)}, u32[]{:S(2)}, u32[]{:S(2)}) collective-permute-start(bf16[1024,128]{1,0:T(8,128)(2,1)S(1)} %pad_maximum_fusion.5), channel_id=1, source_target_pairs={{0,96},{8,104},{16,112},{24,120},{32,0},{40,8},{48,16},{56,24},{64... | collective-permute-start | bytes 786440 | tf_op jit(solution)/shard_map/ppermute | solution.py:239
  20.6 13.0 %collective-permute-start.12 = (bf16[1024,128]{1,0:T(8,128)(2,1)S(1)}, bf16[1024,128]{1,0:T(8,128)(2,1)S(1)}, u32[]{:S(2)}, u32[]{:S(2)}) collective-permute-start(bf16[1024,128]{1,0:T(8,128)(2,1)S(1)} %collective-permute-done.1.refs_3_), channel_id=1, source_target_pairs={{0,112},{8,120},{16,96},{24,104},{32,16},{40,24},{48,0},{56,8},{64... | collective-permute-start | bytes 786440 | tf_op jit(solution)/shard_map/ppermute | solution.py:239
  27.7 12.8 %collective-permute-start.10 = (bf16[1536,128]{1,0:T(8,128)(2,1)S(1)}, bf16[1536,128]{1,0:T(8,128)(2,1)S(1)}, u32[]{:S(2)}, u32[]{:S(2)}) collective-permute-start(bf16[1536,128]{1,0:T(8,128)(2,1)S(1)} %pad_maximum_fusion.2), channel_id=1, source_target_pairs={{0,24},{8,0},{16,8},{24,16},{32,56},{40,32},{48,40},{56,48},{64,88... | collective-permute-start | bytes 1179656 | tf_op jit(solution)/shard_map/ppermute | solution.py:239
  29.1 11.5 %collective-permute-start.11 = (bf16[1536,128]{1,0:T(8,128)(2,1)S(1)}, bf16[1536,128]{1,0:T(8,128)(2,1)S(1)}, u32[]{:S(2)}, u32[]{:S(2)}) collective-permute-start(bf16[1536,128]{1,0:T(8,128)(2,1)S(1)} %pad_maximum_fusion.3), channel_id=1, source_target_pairs={{0,32},{8,40},{16,48},{24,56},{32,64},{40,72},{48,80},{56,88},{64,... | collective-permute-start | bytes 1179656 | tf_op jit(solution)/shard_map/ppermute | solution.py:239
  30.6 14.8 %collective-permute-start.6 = (bf16[1536,128]{1,0:T(8,128)(2,1)S(1)}, bf16[1536,128]{1,0:T(8,128)(2,1)S(1)}, u32[]{:S(2)}, u32[]{:S(2)}) collective-permute-start(bf16[1536,128]{1,0:T(8,128)(2,1)S(1)} %pad_maximum_fusion.1), channel_id=1, source_target_pairs={{0,96},{8,104},{16,112},{24,120},{32,0},{40,8},{48,16},{56,24},{64... | collective-permute-start | bytes 1179656 | tf_op jit(solution)/shard_map/ppermute | solution.py:239
  33.0 12.4 %collective-permute-start.4 = (bf16[1536,128]{1,0:T(8,128)(2,1)S(1)}, bf16[1536,128]{1,0:T(8,128)(2,1)S(1)}, u32[]{:S(2)}, u32[]{:S(2)}) collective-permute-start(bf16[1536,128]{1,0:T(8,128)(2,1)S(1)} %pad_maximum_fusion), channel_id=1, source_target_pairs={{0,8},{8,16},{16,24},{24,0},{32,40},{40,48},{48,56},{56,32},{64,72... | collective-permute-start | bytes 1179656 | tf_op jit(solution)/shard_map/ppermute | solution.py:239
  51.7 5.7 %collective-permute-start.14 = (f32[1,3072]{1,0:T(1,128)S(1)}, f32[1,3072]{1,0:T(1,128)S(1)}, u32[]{:S(2)}, u32[]{:S(2)}) collective-permute-start(f32[1,3072]{1,0:T(1,128)S(1)} %compare_select_fusion.refs_1_), channel_id=1, source_target_pairs={{0,2},{1,3},{2,4},{3,5},{4,6},{5,7},{6,0},{7,1},{8,10},{9,11},{10,... | collective-permute-start | bytes 36872 | tf_op jit(solution)/shard_map/ppermute | solution.py:336
  53.3 5.2 %collective-permute-start.15 = (f32[1,3072]{1,0:T(1,128)S(1)}, f32[1,3072]{1,0:T(1,128)S(1)}, u32[]{:S(2)}, u32[]{:S(2)}) collective-permute-start(f32[1,3072]{1,0:T(1,128)S(1)} %compare_select_fusion.refs_1_), channel_id=1, source_target_pairs={{0,4},{1,5},{2,6},{3,7},{4,0},{5,1},{6,2},{7,3},{8,12},{9,13},{10,... | collective-permute-start | bytes 36872 | tf_op jit(solution)/shard_map/ppermute | solution.py:336
  56.0 3.7 %collective-permute-start.16 = (f32[1,3072]{1,0:T(1,128)S(1)}, f32[1,3072]{1,0:T(1,128)S(1)}, u32[]{:S(2)}, u32[]{:S(2)}) collective-permute-start(f32[1,3072]{1,0:T(1,128)S(1)} %compare_select_fusion.refs_1_), channel_id=1, source_target_pairs={{0,6},{1,7},{2,0},{3,1},{4,2},{5,3},{6,4},{7,5},{8,14},{9,15},{10,... | collective-permute-start | bytes 36872 | tf_op jit(solution)/shard_map/ppermute | solution.py:336
  78.8 5.0 %collective-permute-start.18 = (f32[1,3072]{1,0:T(1,128)S(1)}, f32[1,3072]{1,0:T(1,128)S(1)}, u32[]{:S(2)}, u32[]{:S(2)}) collective-permute-start(f32[1,3072]{1,0:T(1,128)S(1)} %add.22.refs_2_), channel_id=1, source_target_pairs={{0,2},{1,3},{2,4},{3,5},{4,6},{5,7},{6,0},{7,1},{8,10},{9,11},{10,... | collective-permute-start | bytes 36872 | tf_op jit(solution)/shard_map/ppermute | solution.py:336
  79.1 5.6 %collective-permute-start.19 = (f32[1,3072]{1,0:T(1,128)S(1)}, f32[1,3072]{1,0:T(1,128)S(1)}, u32[]{:S(2)}, u32[]{:S(2)}) collective-permute-start(f32[1,3072]{1,0:T(1,128)S(1)} %add.22.refs_2_), channel_id=1, source_target_pairs={{0,4},{1,5},{2,6},{3,7},{4,0},{5,1},{6,2},{7,3},{8,12},{9,13},{10,... | collective-permute-start | bytes 36872 | tf_op jit(solution)/shard_map/ppermute | solution.py:336
  82.9 3.7 %collective-permute-start.20 = (f32[1,3072]{1,0:T(1,128)S(1)}, f32[1,3072]{1,0:T(1,128)S(1)}, u32[]{:S(2)}, u32[]{:S(2)}) collective-permute-start(f32[1,3072]{1,0:T(1,128)S(1)} %add.22.refs_2_), channel_id=1, source_target_pairs={{0,6},{1,7},{2,0},{3,1},{4,2},{5,3},{6,4},{7,5},{8,14},{9,15},{10,... | collective-permute-start | bytes 36872 | tf_op jit(solution)/shard_map/ppermute | solution.py:336
  100.3 1.5 %collective-permute-start.21 = (f32[1,3072]{1,0:T(1,128)S(1)}, f32[1,3072]{1,0:T(1,128)S(1)}, u32[]{:S(2)}, u32[]{:S(2)}) collective-permute-start(f32[1,3072]{1,0:T(1,128)S(1)} %rows.1), channel_id=1, source_target_pairs={{0,1},{1,0},{2,3},{3,2},{4,5},{5,4},{6,7},{7,6},{8,9},{9,8},{10,11... | collective-permute-start | bytes 36872 | tf_op jit(solution)/shard_map/ppermute | solution.py:341
  101.8 5.0 %collective-permute-start.22 = (f32[1,3072]{1,0:T(1,128)S(1)}, f32[1,3072]{1,0:T(1,128)S(1)}, u32[]{:S(2)}, u32[]{:S(2)}) collective-permute-start(f32[1,3072]{1,0:T(1,128)S(1)} %add.23.refs_2_), channel_id=1, source_target_pairs={{0,2},{1,3},{2,4},{3,5},{4,6},{5,7},{6,0},{7,1},{8,10},{9,11},{10,... | collective-permute-start | bytes 36872 | tf_op jit(solution)/shard_map/ppermute | solution.py:336
  101.9 5.3 %collective-permute-start.23 = (f32[1,3072]{1,0:T(1,128)S(1)}, f32[1,3072]{1,0:T(1,128)S(1)}, u32[]{:S(2)}, u32[]{:S(2)}) collective-permute-start(f32[1,3072]{1,0:T(1,128)S(1)} %add.23.refs_2_), channel_id=1, source_target_pairs={{0,4},{1,5},{2,6},{3,7},{4,0},{5,1},{6,2},{7,3},{8,12},{9,13},{10,... | collective-permute-start | bytes 36872 | tf_op jit(solution)/shard_map/ppermute | solution.py:336
  104.6 3.7 %collective-permute-start.24 = (f32[1,3072]{1,0:T(1,128)S(1)}, f32[1,3072]{1,0:T(1,128)S(1)}, u32[]{:S(2)}, u32[]{:S(2)}) collective-permute-start(f32[1,3072]{1,0:T(1,128)S(1)} %add.23.refs_2_), channel_id=1, source_target_pairs={{0,6},{1,7},{2,0},{3,1},{4,2},{5,3},{6,4},{7,5},{8,14},{9,15},{10,... | collective-permute-start | bytes 36872 | tf_op jit(solution)/shard_map/ppermute | solution.py:336
  110.8 11.1 %all-to-all-start.2 = ((f32[16,1,1024]{2,1,0:T(1,128)}), f32[16,1,1024]{2,1,0:T(1,128)S(1)}, u32[]{:S(2)}, u32[]{:S(2)}) async-start(f32[16,1,1024]{2,1,0:T(1,128)} %copy.12), calls=%async_computation.2 | async-start | bytes 131072 | tf_op jit(solution)/shard_map/all_to_all | solution.py:346
  (3 other events, 23.7 us)
where the time goes:
time: 123 us
  Pallas kernels  42.5 us (35%)
  starting transfers between devices  39.8 us (32%)
  blocking collectives  24 us (20%)
  waiting for transfers between devices  13.3 us (11%)
    all_to_all x2, blocking collectives, spread(): return lax.all_to_all(x.reshape(n, 1, -1), 'train', 0, 0).reshape(n, -1)  24 us
    pallas_call x4, Pallas kernels, product_part(): pl.pallas_call(lambda *refs: part_kernel(plan, len(vals), row, tile, alph...  22.3 us
    ppermute x13, starting transfers between devices, from_step(): return lax.ppermute(x, 'train', pairs)  21.8 us
    ppermute x9, starting transfers between devices, other_chips(): lax.ppermute(x, 'val', [(i, (i + 2 * k) % n) for i in range(n)])  14.1 us
    ppermute x9, waiting for transfers between devices, other_chips(): lax.ppermute(x, 'val', [(i, (i + 2 * k) % n) for i in range(n)])  8.2 us
    pallas_call x1, Pallas kernels, shards(): pl.pallas_call(lambda *refs: train_kernel(256, math.log2(total_cols), *re...  6.37 us
    pallas_call x1, Pallas kernels, shards(): pl.pallas_call(lambda *refs: prepare_kernel(features, 512, *refs), out_sh...  4.79 us
    pallas_call x1, Pallas kernels, shards(): pl.pallas_call(lambda *refs: kernel_kernel(math.log2(total_cols), *refs),...  3.57 us
  transfers between devices with their start and end apart: 26, of which 13 were waited for; matrix products, arithmetic and copies ran while one was open for 0% of the time, Pallas kernels for 23%

commit v1 on v0

--- a/solution.py
+++ b/solution.py
@@ -168,7 +168,7 @@
             else:
                 sq[at, :] = total
 
-    @pl.loop(0, rows // tile)
+    @pl.loop(0, rows // tile, unroll=not last)
     def _(k):
         at = pl.ds(pl.multiple_of(k * tile, tile), tile)
         left, right = [], []
@@ -278,7 +278,7 @@
     cols, rows = scores.shape
     pot = log_cols - logsum2([l0[...], l1[...], l2[...], l3[...]])
     row_pot[...] = pot
-    block = 64
+    block = 128
 
     @pl.loop(0, cols // block, unroll=4)
     def _(k):
@@ -303,13 +303,15 @@
     for k in range(cols // 128):
         part = pl.ds(k * 128, 128)
         peaks[:, part] = turn(peak_b[part, :])
-        col_log[:, part] = jnp.broadcast_to(turn(log_b[part, :]), (col_log.shape[0], 128))
+        turned = turn(log_b[part, :])
+        for g in range(col_log.shape[0]):
+            col_log[g, :, part] = turned
 
 
 def first_rows_kernel(total_rows, kern, peaks, col_logs, weights, first_log, sums):
     logs = col_logs[...]
-    peak = jnp.max(logs, axis=0, keepdims=True)
-    whole = peak + jnp.log2(jnp.sum(jnp.exp2(logs - peak), axis=0, keepdims=True))
+    peak = jnp.max(logs, axis=0)
+    whole = peak + jnp.log2(jnp.sum(jnp.exp2(logs - peak[None]), axis=0))
     first_log[...] = whole
     v = jnp.exp2(peaks[...] - whole) * total_rows
     weights[...] = v
@@ -318,7 +320,7 @@
 
 
 def next_rows_kernel(total_rows, kern, weights, col_sums, sums):
-    v = weights[...] * (total_rows / jnp.sum(col_sums[...], axis=0, keepdims=True))
+    v = weights[...] * (total_rows / jnp.sum(col_sums[...], axis=0))
     out = jnp.dot(split_rows(v), kern[...], preferred_element_type=jnp.float32)
     sums[...] = jnp.sum(out, axis=0, keepdims=True)
 
@@ -327,7 +329,8 @@
     u = total_cols / ((r0[...] + r1[...]) + (r2[...] + r3[...]))
     out = lax.dot_general(split_rows(u), kern[...], LAST, preferred_element_type=jnp.float32)
     out = jnp.sum(out, axis=0, keepdims=True) * weights[...]
-    sums[...] = jnp.broadcast_to(out, sums.shape)
+    for g in range(sums.shape[0]):
+        sums[g] = out
 
 
 def other_chips(x):
@@ -342,8 +345,7 @@
 
 
 def spread(x):
-    n = lax.axis_size("train")
-    return lax.all_to_all(x.reshape(n, 1, -1), "train", 0, 0).reshape(n, -1)
+    return lax.all_to_all(x, "train", 0, 0)
 
 
 def shards(train_embed, val_embed, train_labels, val_labels, label_cost):
@@ -382,16 +384,16 @@
     alpha = 2.0 * KAPPA / features
     given = product_part("product_near", near, 0, 1024, train, [label_rows, train_hot])
     scores, squares = product_part("product_diagonal", diagonal, 0, 1024, train, given)
-    scores, log_a = product_part("product_a", last_a, 0, 1024, train, [scores, squares], alpha)
+    scores, log_a = product_part("product_a", last_a, 0, 1536, train, [scores, squares], alpha)
     scores, log_b = product_part(
-        "product_b", last_b, cols // 2, 1024, train, [scores, squares], alpha
+        "product_b", last_b, cols // 2, 1536, train, [scores, squares], alpha
     )
     row_log = jnp.logaddexp2(log_a, log_b)
 
     both = jnp.logaddexp2(row_log, other_core(row_log))
     kern, row_pot, peaks, col_log = pl.pallas_call(
         lambda *refs: kernel_kernel(math.log2(total_cols), *refs),
-        out_shape=(shape_of((cols, rows), jnp.bfloat16), vec_r, vec_c, shape_of((groups, cols))),
+        out_shape=(shape_of((cols, rows), jnp.bfloat16), vec_r, vec_c, shape_of((groups, 1, cols))),
         in_specs=[VMEM] * 5,
         out_specs=(VMEM,) * 4,
         scratch_shapes=[pltpu.VMEM((cols, 128), jnp.float32)] * 2,
@@ -413,7 +415,7 @@
         others = other_chips(both)
         col_sums = pl.pallas_call(
             lambda *refs: cols_kernel(total_cols, *refs),
-            out_shape=shape_of((groups, cols)),
+            out_shape=shape_of((groups, 1, cols)),
             in_specs=[VMEM] * 6,
             out_specs=VMEM,
             compiler_params=params(SMALL),
@@ -443,7 +445,7 @@
         compiler_params=params(14),
         name="train_potential",
     )(in_hbm(train_embed), row_pot, both, *others).reshape(rows)
-    col_total = jnp.sum(col_sums, axis=0, keepdims=True)
+    col_total = jnp.sum(col_sums, axis=0)
     val_potential = ((2.0 * math.log2(total_rows) - first_log) - jnp.log2(col_total)) / KAPPA
     return train_potential, val_potential.reshape(cols)
 

time: 123 us -> 121 us (0.984)
    pallas_call x4, Pallas kernels: 22.3 us -> 20.8 us  [product_part(): pl.pallas_call(lambda *refs: part_kernel(plan, len(vals), row, tile, alph...]
  transfers between devices with their start and end apart: 26 -> 26, of which waited for: 13 -> 14; matrix products, arithmetic and copies ran while one was open for 0% -> 0% of each run, Pallas kernels for 23% -> 23%
where the time goes in v1:
time: 121 us
  Pallas kernels  41.3 us (34%)
  starting transfers between devices  40 us (33%)
  blocking collectives  24 us (20%)
  waiting for transfers between devices  13.4 us (11%)
    all_to_all x2, blocking collectives, spread(): return lax.all_to_all(x, 'train', 0, 0)  24 us
    ppermute x13, starting transfers between devices, from_step(): return lax.ppermute(x, 'train', pairs)  22.1 us
    pallas_call x4, Pallas kernels, product_part(): pl.pallas_call(lambda *refs: part_kernel(plan, len(vals), row, tile, alph...  20.8 us
    ppermute x9, starting transfers between devices, other_chips(): lax.ppermute(x, 'val', [(i, (i + 2 * k) % n) for i in range(n)])  14.1 us
    ppermute x9, waiting for transfers between devices, other_chips(): lax.ppermute(x, 'val', [(i, (i + 2 * k) % n) for i in range(n)])  8.19 us
    pallas_call x1, Pallas kernels, shards(): pl.pallas_call(lambda *refs: train_kernel(256, math.log2(total_cols), *re...  6.37 us
    pallas_call x1, Pallas kernels, shards(): pl.pallas_call(lambda *refs: prepare_kernel(features, 512, *refs), out_sh...  4.79 us
    pallas_call x2, Pallas kernels, shards(): pl.pallas_call(lambda *refs: cols_kernel(total_cols, *refs), out_shape=sh...  4.13 us
  transfers between devices with their start and end apart: 26, of which 14 were waited for; matrix products, arithmetic and copies ran while one was open for 0% of the time, Pallas kernels for 23%

profile of v1, /device:TPU:0, one launch (start us, length us, event | category | flops | bytes accessed | tf_op | source)
XLA Modules:
  0.0 120.8 jit_solution(15638675827061417522)
XLA Ops:
  0.6 3.2 %collective-permute-start.1 = (bf16[1024,128]{1,0:T(8,128)(2,1)}, bf16[1024,128]{1,0:T(8,128)(2,1)S(1)}, u32[]{:S(2)}, u32[]{:S(2)}) collective-permute-start(bf16[1024,128]{1,0:T(8,128)(2,1)} %refs_0_.4), channel_id=1, source_target_pairs={{0,96},{8,104},{16,112},{24,120},{32,0},{40,8},{48,16},{56,24},{64... | collective-permute-start | bytes 786440 | tf_op jit(solution)/shard_map/ppermute | solution.py:239
  3.8 1.9 %collective-permute-start = (bf16[1024,128]{1,0:T(8,128)(2,1)}, bf16[1024,128]{1,0:T(8,128)(2,1)S(1)}, u32[]{:S(2)}, u32[]{:S(2)}) collective-permute-start(bf16[1024,128]{1,0:T(8,128)(2,1)} %refs_0_.4), channel_id=1, source_target_pairs={{0,8},{8,16},{16,24},{24,0},{32,40},{40,48},{48,56},{56,32},{64,72... | collective-permute-start | bytes 786440 | tf_op jit(solution)/shard_map/ppermute | solution.py:239
  5.7 2.1 %collective-permute-start.7 = (bf16[1024,128]{1,0:T(8,128)(2,1)}, bf16[1024,128]{1,0:T(8,128)(2,1)S(1)}, u32[]{:S(2)}, u32[]{:S(2)}) collective-permute-start(bf16[1024,128]{1,0:T(8,128)(2,1)} %refs_0_.4), channel_id=1, source_target_pairs={{0,24},{8,0},{16,8},{24,16},{32,56},{40,32},{48,40},{56,48},{64,88... | collective-permute-start | bytes 786440 | tf_op jit(solution)/shard_map/ppermute | solution.py:239
  7.9 4.8 %prepare.1 = (bf16[3072,2048]{1,0:T(8,128)(2,1)S(1)}, bf16[3072,128]{1,0:T(8,128)(2,1)S(1)}, bf16[1024,128]{1,0:T(8,128)(2,1)S(1)}) custom-call(f32[10,10]{1,0:T(8,128)} %refs_0_.3, s32[1,3072]{1,0:T(1,128)} %bitcast.6, s32[1,1024]{1,0:T(1,128)} %bitcast.8, bf16[3072,2048]{1,0:T(8,128)(2,1)} %refs_0_.5), custom_call_target="tpu_custom_call" | custom-call | tf_op jit(solution)/shard_map/prepare/pallas_call | solution.py:360
  13.0 2.0 %collective-permute-start.3 = (bf16[1024,128]{1,0:T(8,128)(2,1)S(1)}, bf16[1024,128]{1,0:T(8,128)(2,1)S(1)}, u32[]{:S(2)}, u32[]{:S(2)}) collective-permute-start(bf16[1024,128]{1,0:T(8,128)(2,1)S(1)} %pad_maximum_fusion.4), channel_id=1, source_target_pairs={{0,8},{8,16},{16,24},{24,0},{32,40},{40,48},{48,56},{56,32},{64,72... | collective-permute-start | bytes 786440 | tf_op jit(solution)/shard_map/ppermute | solution.py:239
  15.0 2.2 %collective-permute-start.5 = (bf16[1024,128]{1,0:T(8,128)(2,1)S(1)}, bf16[1024,128]{1,0:T(8,128)(2,1)S(1)}, u32[]{:S(2)}, u32[]{:S(2)}) collective-permute-start(bf16[1024,128]{1,0:T(8,128)(2,1)S(1)} %pad_maximum_fusion.4), channel_id=1, source_target_pairs={{0,24},{8,0},{16,8},{24,16},{32,56},{40,32},{48,40},{56,48},{64,88... | collective-permute-start | bytes 786440 | tf_op jit(solution)/shard_map/ppermute | solution.py:239
  17.4 3.2 %collective-permute-start.8 = (bf16[1024,128]{1,0:T(8,128)(2,1)S(1)}, bf16[1024,128]{1,0:T(8,128)(2,1)S(1)}, u32[]{:S(2)}, u32[]{:S(2)}) collective-permute-start(bf16[1024,128]{1,0:T(8,128)(2,1)S(1)} %pad_maximum_fusion.5), channel_id=1, source_target_pairs={{0,96},{8,104},{16,112},{24,120},{32,0},{40,8},{48,16},{56,24},{64... | collective-permute-start | bytes 786440 | tf_op jit(solution)/shard_map/ppermute | solution.py:239
  21.8 5.2 %product_near.1 = (f32[1024,3072]{1,0:T(8,128)S(1)}, f32[1024,128]{1,0:T(8,128)S(1)}) custom-call(bf16[1024,128]{1,0:T(8,128)(2,1)S(1)} %copy-done, bf16[1024,128]{1,0:T(8,128)(2,1)S(1)} %collective-permute-done.7.refs_1_, bf16[1024,128]{1,0:T(8,128)(2,1)S(1)} %collective-permute-done.refs_2_, bf16[1024,128]{1,0:T(8,128)(2,1)S(1)} %collective-permute-done.1.refs_3_, ...), custom_call_target="tpu_custom_call" | custom-call | flops 4026531840 | tf_op jit(solution)/shard_map/product_near/pallas_call | solution.py:218
  27.3 1.7 %collective-permute-start.10 = (bf16[1536,128]{1,0:T(8,128)(2,1)S(1)}, bf16[1536,128]{1,0:T(8,128)(2,1)S(1)}, u32[]{:S(2)}, u32[]{:S(2)}) collective-permute-start(bf16[1536,128]{1,0:T(8,128)(2,1)S(1)} %pad_maximum_fusion.2), channel_id=1, source_target_pairs={{0,24},{8,0},{16,8},{24,16},{32,56},{40,32},{48,40},{56,48},{64,88... | collective-permute-start | bytes 1179656 | tf_op jit(solution)/shard_map/ppermute | solution.py:239
  30.1 2.9 %collective-permute-start.6 = (bf16[1536,128]{1,0:T(8,128)(2,1)S(1)}, bf16[1536,128]{1,0:T(8,128)(2,1)S(1)}, u32[]{:S(2)}, u32[]{:S(2)}) collective-permute-start(bf16[1536,128]{1,0:T(8,128)(2,1)S(1)} %pad_maximum_fusion.1), channel_id=1, source_target_pairs={{0,96},{8,104},{16,112},{24,120},{32,0},{40,8},{48,16},{56,24},{64... | collective-permute-start | bytes 1179656 | tf_op jit(solution)/shard_map/ppermute | solution.py:239
  33.6 6.3 %product_diagonal.1 = (f32[1024,3072]{1,0:T(8,128)S(1)}, f32[1024,128]{1,0:T(8,128)S(1)}) custom-call(bf16[1024,128]{1,0:T(8,128)(2,1)S(1)} %collective-permute-done.8.refs_0_, bf16[1024,128]{1,0:T(8,128)(2,1)S(1)} %collective-permute-done.5.refs_1_, bf16[1024,128]{1,0:T(8,128)(2,1)S(1)} %collective-permute-done.3.refs_2_, ...), custom_call_target="tpu_custom_call", output_to_operand_aliasing={{0}: (6, {})} | custom-call | flops 4026531840 | tf_op jit(solution)/shard_map/product_diagonal/pallas_call | solution.py:218
  40.0 4.6 %product_a.1 = (f32[1024,3072]{1,0:T(8,128)S(1)}, f32[1,3072]{1,0:T(1,128)S(1)}) custom-call(bf16[1536,128]{1,0:T(8,128)(2,1)S(1)} %collective-permute-done.10.refs_0_, bf16[1536,128]{1,0:T(8,128)(2,1)S(1)} %collective-permute-done.11.refs_1_, bf16[3072,2048]{1,0:T(8,128)(2,1)S(1)} %get-tuple-element.20.refs_5_.refs_2_, ...), custom_call_target="tpu_custom_call", output_to_operand_aliasing={{0}: (3, {})} | custom-call | flops 2415919104 | tf_op jit(solution)/shard_map/product_a/pallas_call | solution.py:218
  44.7 4.6 %product_b.1 = (f32[1024,3072]{1,0:T(8,128)S(1)}, f32[1,3072]{1,0:T(1,128)S(1)}) custom-call(bf16[1536,128]{1,0:T(8,128)(2,1)S(1)} %collective-permute-done.4.refs_0_, bf16[1536,128]{1,0:T(8,128)(2,1)S(1)} %collective-permute-done.6.refs_1_, bf16[3072,2048]{1,0:T(8,128)(2,1)S(1)} %get-tuple-element.20.refs_5_.refs_2_, ...), custom_call_target="tpu_custom_call", output_to_operand_aliasing={{0}: (3, {})} | custom-call | flops 2415919104 | tf_op jit(solution)/shard_map/product_b/pallas_call | solution.py:218
  52.3 2.8 %collective-permute-start.15 = (f32[1,3072]{1,0:T(1,128)S(1)}, f32[1,3072]{1,0:T(1,128)S(1)}, u32[]{:S(2)}, u32[]{:S(2)}) collective-permute-start(f32[1,3072]{1,0:T(1,128)S(1)} %compare_select_fusion.refs_1_), channel_id=1, source_target_pairs={{0,4},{1,5},{2,6},{3,7},{4,0},{5,1},{6,2},{7,3},{8,12},{9,13},{10,... | collective-permute-start | bytes 36872 | tf_op jit(solution)/shard_map/ppermute | solution.py:339
  58.7 3.2 %kernel_matrix.1 = (bf16[1024,3072]{1,0:T(8,128)(2,1)S(1)}, f32[1,3072]{1,0:T(1,128)S(1)}, f32[1,1024]{1,0:T(1,128)S(1)}, f32[16,1,1024]{2,1,0:T(1,128)S(1)}) custom-call(f32[1024,3072]{1,0:T(8,128)S(1)} %get-tuple-element.28.refs_0_, f32[1,3072]{1,0:T(1,128)S(1)} %compare_select_fusion.refs_1_, f32[1,3072]{1,0:T(1,128)S(1)} %collective-permute-done.14.refs_2_, ...), custom_call_target="tpu_custom_call" | custom-call | tf_op jit(solution)/shard_map/kernel_matrix/pallas_call | solution.py:394
  62.0 13.1 %all_to_all.15.refs_2_ = f32[16,1,1024]{2,1,0:T(1,128)S(1)} all-to-all(f32[16,1,1024]{2,1,0:T(1,128)S(1)} %get-tuple-element.34), channel_id=1, replica_groups=mesh['train'=16,'val'=8] {'train'}, dimensions={0} | all-to-all | bytes 131072 | tf_op jit(solution)/shard_map/all_to_all | solution.py:348
  77.7 3.8 %collective-permute-start.19 = (f32[1,3072]{1,0:T(1,128)S(1)}, f32[1,3072]{1,0:T(1,128)S(1)}, u32[]{:S(2)}, u32[]{:S(2)}) collective-permute-start(f32[1,3072]{1,0:T(1,128)S(1)} %add.22.refs_2_), channel_id=1, source_target_pairs={{0,4},{1,5},{2,6},{3,7},{4,0},{5,1},{6,2},{7,3},{8,12},{9,13},{10,... | collective-permute-start | bytes 36872 | tf_op jit(solution)/shard_map/ppermute | solution.py:339
  83.3 1.9 %collective-permute-done.20.refs_5_ = f32[1,3072]{1,0:T(1,128)S(1)} collective-permute-done((f32[1,3072]{1,0:T(1,128)S(1)}, f32[1,3072]{1,0:T(1,128)S(1)}, u32[]{:S(2)}, u32[]{:S(2)}) %collective-permute-start.20) | collective-permute-done | bytes 12320 | tf_op jit(solution)/shard_map/ppermute | solution.py:339
  85.2 1.8 %columns.2 = f32[16,1,1024]{2,1,0:T(1,128)S(1)} custom-call(bf16[1024,3072]{1,0:T(8,128)(2,1)S(1)} %get-tuple-element.32.refs_0_, f32[1,1024]{1,0:T(1,128)S(1)} %get-tuple-element.35.refs_1_, f32[1,3072]{1,0:T(1,128)S(1)} %add.22.refs_2_, f32[1,3072]{1,0:T(1,128)S(1)} %collective-permute-done.18.refs_3_, f32[1,3072]{1,0:T(1,128)S(1)} %collective-permute-done.19.refs_4_, ...), custom_call_target="tpu_custom_call" | custom-call | tf_op jit(solution)/shard_map/columns/pallas_call | solution.py:416
  87.0 10.9 %all_to_all.16.refs_2_ = f32[16,1,1024]{2,1,0:T(1,128)S(1)} all-to-all(f32[16,1,1024]{2,1,0:T(1,128)S(1)} %columns.2), channel_id=1, replica_groups=mesh['train'=16,'val'=8] {'train'}, dimensions={0} | all-to-all | bytes 131072 | tf_op jit(solution)/shard_map/all_to_all | solution.py:348
  100.3 2.7 %collective-permute-start.23 = (f32[1,3072]{1,0:T(1,128)S(1)}, f32[1,3072]{1,0:T(1,128)S(1)}, u32[]{:S(2)}, u32[]{:S(2)}) collective-permute-start(f32[1,3072]{1,0:T(1,128)S(1)} %add.23.refs_2_), channel_id=1, source_target_pairs={{0,4},{1,5},{2,6},{3,7},{4,0},{5,1},{6,2},{7,3},{8,12},{9,13},{10,... | collective-permute-start | bytes 36872 | tf_op jit(solution)/shard_map/ppermute | solution.py:339
  106.6 2.4 %columns.3 = f32[16,1,1024]{2,1,0:T(1,128)} custom-call(bf16[1024,3072]{1,0:T(8,128)(2,1)S(1)} %get-tuple-element.32.refs_0_, f32[1,1024]{1,0:T(1,128)S(1)} %get-tuple-element.35.refs_1_, f32[1,3072]{1,0:T(1,128)S(1)} %add.23.refs_2_, f32[1,3072]{1,0:T(1,128)S(1)} %collective-permute-done.22.refs_3_, f32[1,3072]{1,0:T(1,128)S(1)} %collective-permute-done.23.refs_4_, ...), custom_call_target="tpu_custom_call" | custom-call | tf_op jit(solution)/shard_map/columns/pallas_call | solution.py:416
  109.0 3.5 %all-to-all-start.2 = ((f32[16,1,1024]{2,1,0:T(1,128)}), f32[16,1,1024]{2,1,0:T(1,128)S(1)}, u32[]{:S(2)}, u32[]{:S(2)}) async-start(f32[16,1,1024]{2,1,0:T(1,128)} %columns.3), calls=%async_computation.2 | async-start | bytes 131072 | tf_op jit(solution)/shard_map/all_to_all | solution.py:348
  112.5 6.4 %train_potential.1 = f32[1,3072]{1,0:T(1,128)} custom-call(bf16[3072,2048]{1,0:T(8,128)(2,1)} %refs_0_.5, f32[1,3072]{1,0:T(1,128)S(1)} %get-tuple-element.31.refs_1_, f32[1,3072]{1,0:T(1,128)S(1)} %add.23.refs_2_, f32[1,3072]{1,0:T(1,128)S(1)} %collective-permute-done.22.refs_3_, f32[1,3072]{1,0:T(1,128)S(1)} %collective-permute-done.23.refs_4_, ...), custom_call_target="tpu_custom_call" | custom-call | tf_op jit(solution)/shard_map/train_potential/pallas_call | solution.py:435
  (64 shorter events, 22.7 us)
Async XLA Ops:
  0.6 12.0 %collective-permute-start.1 = (bf16[1024,128]{1,0:T(8,128)(2,1)}, bf16[1024,128]{1,0:T(8,128)(2,1)S(1)}, u32[]{:S(2)}, u32[]{:S(2)}) collective-permute-start(bf16[1024,128]{1,0:T(8,128)(2,1)} %refs_0_.4), channel_id=1, source_target_pairs={{0,96},{8,104},{16,112},{24,120},{32,0},{40,8},{48,16},{56,24},{64... | collective-permute-start | bytes 786440 | tf_op jit(solution)/shard_map/ppermute | solution.py:239
  3.8 9.2 %collective-permute-start.2 = (bf16[1024,128]{1,0:T(8,128)(2,1)}, bf16[1024,128]{1,0:T(8,128)(2,1)S(1)}, u32[]{:S(2)}, u32[]{:S(2)}) collective-permute-start(bf16[1024,128]{1,0:T(8,128)(2,1)} %refs_0_.4), channel_id=1, source_target_pairs={{0,32},{8,40},{16,48},{24,56},{32,64},{40,72},{48,80},{56,88},{64,... | collective-permute-start | bytes 786440 | tf_op jit(solution)/shard_map/ppermute | solution.py:239
  3.8 13.4 %collective-permute-start = (bf16[1024,128]{1,0:T(8,128)(2,1)}, bf16[1024,128]{1,0:T(8,128)(2,1)S(1)}, u32[]{:S(2)}, u32[]{:S(2)}) collective-permute-start(bf16[1024,128]{1,0:T(8,128)(2,1)} %refs_0_.4), channel_id=1, source_target_pairs={{0,8},{8,16},{16,24},{24,0},{32,40},{40,48},{48,56},{56,32},{64,72... | collective-permute-start | bytes 786440 | tf_op jit(solution)/shard_map/ppermute | solution.py:239
  5.7 11.5 %collective-permute-start.7 = (bf16[1024,128]{1,0:T(8,128)(2,1)}, bf16[1024,128]{1,0:T(8,128)(2,1)S(1)}, u32[]{:S(2)}, u32[]{:S(2)}) collective-permute-start(bf16[1024,128]{1,0:T(8,128)(2,1)} %refs_0_.4), channel_id=1, source_target_pairs={{0,24},{8,0},{16,8},{24,16},{32,56},{40,32},{48,40},{56,48},{64,88... | collective-permute-start | bytes 786440 | tf_op jit(solution)/shard_map/ppermute | solution.py:239
  13.0 17.0 %collective-permute-start.3 = (bf16[1024,128]{1,0:T(8,128)(2,1)S(1)}, bf16[1024,128]{1,0:T(8,128)(2,1)S(1)}, u32[]{:S(2)}, u32[]{:S(2)}) collective-permute-start(bf16[1024,128]{1,0:T(8,128)(2,1)S(1)} %pad_maximum_fusion.4), channel_id=1, source_target_pairs={{0,8},{8,16},{16,24},{24,0},{32,40},{40,48},{48,56},{56,32},{64,72... | collective-permute-start | bytes 786440 | tf_op jit(solution)/shard_map/ppermute | solution.py:239
  15.0 15.0 %collective-permute-start.5 = (bf16[1024,128]{1,0:T(8,128)(2,1)S(1)}, bf16[1024,128]{1,0:T(8,128)(2,1)S(1)}, u32[]{:S(2)}, u32[]{:S(2)}) collective-permute-start(bf16[1024,128]{1,0:T(8,128)(2,1)S(1)} %pad_maximum_fusion.4), channel_id=1, source_target_pairs={{0,24},{8,0},{16,8},{24,16},{32,56},{40,32},{48,40},{56,48},{64,88... | collective-permute-start | bytes 786440 | tf_op jit(solution)/shard_map/ppermute | solution.py:239
  17.3 9.7 %collective-permute-start.9 = (bf16[1024,128]{1,0:T(8,128)(2,1)S(1)}, bf16[1024,128]{1,0:T(8,128)(2,1)S(1)}, u32[]{:S(2)}, u32[]{:S(2)}) collective-permute-start(bf16[1024,128]{1,0:T(8,128)(2,1)S(1)} %pad_maximum_fusion.5), channel_id=1, source_target_pairs={{0,32},{8,40},{16,48},{24,56},{32,64},{40,72},{48,80},{56,88},{64,... | collective-permute-start | bytes 786440 | tf_op jit(solution)/shard_map/ppermute | solution.py:239
  17.4 9.8 %collective-permute-start.8 = (bf16[1024,128]{1,0:T(8,128)(2,1)S(1)}, bf16[1024,128]{1,0:T(8,128)(2,1)S(1)}, u32[]{:S(2)}, u32[]{:S(2)}) collective-permute-start(bf16[1024,128]{1,0:T(8,128)(2,1)S(1)} %pad_maximum_fusion.5), channel_id=1, source_target_pairs={{0,96},{8,104},{16,112},{24,120},{32,0},{40,8},{48,16},{56,24},{64... | collective-permute-start | bytes 786440 | tf_op jit(solution)/shard_map/ppermute | solution.py:239
  20.6 13.0 %collective-permute-start.12 = (bf16[1024,128]{1,0:T(8,128)(2,1)S(1)}, bf16[1024,128]{1,0:T(8,128)(2,1)S(1)}, u32[]{:S(2)}, u32[]{:S(2)}) collective-permute-start(bf16[1024,128]{1,0:T(8,128)(2,1)S(1)} %collective-permute-done.1.refs_3_), channel_id=1, source_target_pairs={{0,112},{8,120},{16,96},{24,104},{32,16},{40,24},{48,0},{56,8},{64... | collective-permute-start | bytes 786440 | tf_op jit(solution)/shard_map/ppermute | solution.py:239
  27.3 12.7 %collective-permute-start.10 = (bf16[1536,128]{1,0:T(8,128)(2,1)S(1)}, bf16[1536,128]{1,0:T(8,128)(2,1)S(1)}, u32[]{:S(2)}, u32[]{:S(2)}) collective-permute-start(bf16[1536,128]{1,0:T(8,128)(2,1)S(1)} %pad_maximum_fusion.2), channel_id=1, source_target_pairs={{0,24},{8,0},{16,8},{24,16},{32,56},{40,32},{48,40},{56,48},{64,88... | collective-permute-start | bytes 1179656 | tf_op jit(solution)/shard_map/ppermute | solution.py:239
  29.1 10.9 %collective-permute-start.11 = (bf16[1536,128]{1,0:T(8,128)(2,1)S(1)}, bf16[1536,128]{1,0:T(8,128)(2,1)S(1)}, u32[]{:S(2)}, u32[]{:S(2)}) collective-permute-start(bf16[1536,128]{1,0:T(8,128)(2,1)S(1)} %pad_maximum_fusion.3), channel_id=1, source_target_pairs={{0,32},{8,40},{16,48},{24,56},{32,64},{40,72},{48,80},{56,88},{64,... | collective-permute-start | bytes 1179656 | tf_op jit(solution)/shard_map/ppermute | solution.py:239
  30.1 14.5 %collective-permute-start.6 = (bf16[1536,128]{1,0:T(8,128)(2,1)S(1)}, bf16[1536,128]{1,0:T(8,128)(2,1)S(1)}, u32[]{:S(2)}, u32[]{:S(2)}) collective-permute-start(bf16[1536,128]{1,0:T(8,128)(2,1)S(1)} %pad_maximum_fusion.1), channel_id=1, source_target_pairs={{0,96},{8,104},{16,112},{24,120},{32,0},{40,8},{48,16},{56,24},{64... | collective-permute-start | bytes 1179656 | tf_op jit(solution)/shard_map/ppermute | solution.py:239
  33.0 11.6 %collective-permute-start.4 = (bf16[1536,128]{1,0:T(8,128)(2,1)S(1)}, bf16[1536,128]{1,0:T(8,128)(2,1)S(1)}, u32[]{:S(2)}, u32[]{:S(2)}) collective-permute-start(bf16[1536,128]{1,0:T(8,128)(2,1)S(1)} %pad_maximum_fusion), channel_id=1, source_target_pairs={{0,8},{8,16},{16,24},{24,0},{32,40},{40,48},{48,56},{56,32},{64,72... | collective-permute-start | bytes 1179656 | tf_op jit(solution)/shard_map/ppermute | solution.py:239
  49.4 1.3 %collective-permute-start.13 = (f32[1,3072]{1,0:T(1,128)S(1)}, f32[1,3072]{1,0:T(1,128)S(1)}, u32[]{:S(2)}, u32[]{:S(2)}) collective-permute-start(f32[1,3072]{1,0:T(1,128)S(1)} %compare_select_fusion.1), channel_id=1, source_target_pairs={{0,1},{1,0},{2,3},{3,2},{4,5},{5,4},{6,7},{7,6},{8,9},{9,8},{10,11... | collective-permute-start | bytes 36872 | tf_op jit(solution)/shard_map/ppermute | solution.py:344
  50.7 5.7 %collective-permute-start.14 = (f32[1,3072]{1,0:T(1,128)S(1)}, f32[1,3072]{1,0:T(1,128)S(1)}, u32[]{:S(2)}, u32[]{:S(2)}) collective-permute-start(f32[1,3072]{1,0:T(1,128)S(1)} %compare_select_fusion.refs_1_), channel_id=1, source_target_pairs={{0,2},{1,3},{2,4},{3,5},{4,6},{5,7},{6,0},{7,1},{8,10},{9,11},{10,... | collective-permute-start | bytes 36872 | tf_op jit(solution)/shard_map/ppermute | solution.py:339
  52.3 5.2 %collective-permute-start.15 = (f32[1,3072]{1,0:T(1,128)S(1)}, f32[1,3072]{1,0:T(1,128)S(1)}, u32[]{:S(2)}, u32[]{:S(2)}) collective-permute-start(f32[1,3072]{1,0:T(1,128)S(1)} %compare_select_fusion.refs_1_), channel_id=1, source_target_pairs={{0,4},{1,5},{2,6},{3,7},{4,0},{5,1},{6,2},{7,3},{8,12},{9,13},{10,... | collective-permute-start | bytes 36872 | tf_op jit(solution)/shard_map/ppermute | solution.py:339
  55.0 3.7 %collective-permute-start.16 = (f32[1,3072]{1,0:T(1,128)S(1)}, f32[1,3072]{1,0:T(1,128)S(1)}, u32[]{:S(2)}, u32[]{:S(2)}) collective-permute-start(f32[1,3072]{1,0:T(1,128)S(1)} %compare_select_fusion.refs_1_), channel_id=1, source_target_pairs={{0,6},{1,7},{2,0},{3,1},{4,2},{5,3},{6,4},{7,5},{8,14},{9,15},{10,... | collective-permute-start | bytes 36872 | tf_op jit(solution)/shard_map/ppermute | solution.py:339
  77.3 5.0 %collective-permute-start.18 = (f32[1,3072]{1,0:T(1,128)S(1)}, f32[1,3072]{1,0:T(1,128)S(1)}, u32[]{:S(2)}, u32[]{:S(2)}) collective-permute-start(f32[1,3072]{1,0:T(1,128)S(1)} %add.22.refs_2_), channel_id=1, source_target_pairs={{0,2},{1,3},{2,4},{3,5},{4,6},{5,7},{6,0},{7,1},{8,10},{9,11},{10,... | collective-permute-start | bytes 36872 | tf_op jit(solution)/shard_map/ppermute | solution.py:339
  77.7 5.6 %collective-permute-start.19 = (f32[1,3072]{1,0:T(1,128)S(1)}, f32[1,3072]{1,0:T(1,128)S(1)}, u32[]{:S(2)}, u32[]{:S(2)}) collective-permute-start(f32[1,3072]{1,0:T(1,128)S(1)} %add.22.refs_2_), channel_id=1, source_target_pairs={{0,4},{1,5},{2,6},{3,7},{4,0},{5,1},{6,2},{7,3},{8,12},{9,13},{10,... | collective-permute-start | bytes 36872 | tf_op jit(solution)/shard_map/ppermute | solution.py:339
  81.5 3.7 %collective-permute-start.20 = (f32[1,3072]{1,0:T(1,128)S(1)}, f32[1,3072]{1,0:T(1,128)S(1)}, u32[]{:S(2)}, u32[]{:S(2)}) collective-permute-start(f32[1,3072]{1,0:T(1,128)S(1)} %add.22.refs_2_), channel_id=1, source_target_pairs={{0,6},{1,7},{2,0},{3,1},{4,2},{5,3},{6,4},{7,5},{8,14},{9,15},{10,... | collective-permute-start | bytes 36872 | tf_op jit(solution)/shard_map/ppermute | solution.py:339
  100.2 5.0 %collective-permute-start.22 = (f32[1,3072]{1,0:T(1,128)S(1)}, f32[1,3072]{1,0:T(1,128)S(1)}, u32[]{:S(2)}, u32[]{:S(2)}) collective-permute-start(f32[1,3072]{1,0:T(1,128)S(1)} %add.23.refs_2_), channel_id=1, source_target_pairs={{0,2},{1,3},{2,4},{3,5},{4,6},{5,7},{6,0},{7,1},{8,10},{9,11},{10,... | collective-permute-start | bytes 36872 | tf_op jit(solution)/shard_map/ppermute | solution.py:339
  100.3 5.3 %collective-permute-start.23 = (f32[1,3072]{1,0:T(1,128)S(1)}, f32[1,3072]{1,0:T(1,128)S(1)}, u32[]{:S(2)}, u32[]{:S(2)}) collective-permute-start(f32[1,3072]{1,0:T(1,128)S(1)} %add.23.refs_2_), channel_id=1, source_target_pairs={{0,4},{1,5},{2,6},{3,7},{4,0},{5,1},{6,2},{7,3},{8,12},{9,13},{10,... | collective-permute-start | bytes 36872 | tf_op jit(solution)/shard_map/ppermute | solution.py:339
  102.9 3.7 %collective-permute-start.24 = (f32[1,3072]{1,0:T(1,128)S(1)}, f32[1,3072]{1,0:T(1,128)S(1)}, u32[]{:S(2)}, u32[]{:S(2)}) collective-permute-start(f32[1,3072]{1,0:T(1,128)S(1)} %add.23.refs_2_), channel_id=1, source_target_pairs={{0,6},{1,7},{2,0},{3,1},{4,2},{5,3},{6,4},{7,5},{8,14},{9,15},{10,... | collective-permute-start | bytes 36872 | tf_op jit(solution)/shard_map/ppermute | solution.py:339
  109.0 11.1 %all-to-all-start.2 = ((f32[16,1,1024]{2,1,0:T(1,128)}), f32[16,1,1024]{2,1,0:T(1,128)S(1)}, u32[]{:S(2)}, u32[]{:S(2)}) async-start(f32[16,1,1024]{2,1,0:T(1,128)} %columns.3), calls=%async_computation.2 | async-start | bytes 131072 | tf_op jit(solution)/shard_map/all_to_all | solution.py:348
  (3 other events, 23.7 us)

commit v2 on v1

--- a/solution.py
+++ b/solution.py
@@ -52,6 +52,16 @@
     for r in rows[1:]:
         total = total + jnp.exp2(r - peak)
     return peak + jnp.log2(total)
+
+
+def lane_sums(x):
+    ones = jnp.ones((SPLITS, 128), jnp.bfloat16)
+    total = 0.0
+    for _ in range(3):
+        part = x.astype(jnp.bfloat16)
+        x = x - part.astype(jnp.float32)
+        total = total + lax.dot_general(ones, part, LAST, preferred_element_type=jnp.float32)
+    return total[0:1, :]
 
 
 def turn(block):
@@ -77,7 +87,7 @@
         pltpu.make_async_copy(val_labels, more_labels, label_sems.at[1]),
         pltpu.make_async_copy(label_cost, costs, label_sems.at[2]),
     ]
-    spans = [pl.ds(k * tile, tile) for k in range(train.shape[0] // tile)]
+    spans = [pl.ds(k * tile, tile) for k in range(sems.shape[0])]
     copies = [
         pltpu.make_async_copy(source.at[at], train.at[at], sems.at[k]) for k, at in enumerate(spans)
     ]
@@ -124,22 +134,22 @@
                 piece = buf[lax.rem(k, depth), pl.ds(r, 64), pl.ds(c * 128, 128)].astype(jnp.float32)
                 total = total + piece * piece
             squares[pl.ds(pl.multiple_of(k * tile + r, 64), 64), :] = total
-    ones = jnp.ones((SPLITS, 128), jnp.bfloat16)
-    rest, norm = squares[...], 0.0
-    for _ in range(3):
-        part = rest.astype(jnp.bfloat16)
-        rest = rest - part.astype(jnp.float32)
-        norm = norm + lax.dot_general(ones, part, LAST, preferred_element_type=jnp.float32)
+    norm = lane_sums(squares[...])
     total = (r0[...] + r1[...]) + (r2[...] + r3[...])
     pot = (row_pot[...] + (log_cols - jnp.log2(total))) * (1.0 / KAPPA)
-    out[...] = pot + norm[0:1, :] * (1.0 / features)
-
-
-def part_kernel(plan, count, row, tile, alpha, *refs):
+    out[...] = pot + norm * (1.0 / features)
+
+
+def part_kernel(plan, count, row, tile, alpha, early, *refs):
     vals, (train, *given), results = refs[:count], refs[count : count + 3], refs[count + 3 :]
-    first, last = given[0].dtype == jnp.bfloat16, alpha is not None
+    first, last = early is not None, alpha is not None
     if first:
         label_rows, train_hot = given
+        source, *results = results
+        more_train, sem = results[2:]
+        span = pl.ds(early, train.shape[0] - early)
+        copy = pltpu.make_async_copy(source.at[span], more_train.at[span], sem)
+        copy.start()
     else:
         before, sq_before = given
     scores, out = results[:2]
@@ -168,14 +178,18 @@
             else:
                 sq[at, :] = total
 
-    @pl.loop(0, rows // tile, unroll=not last)
-    def _(k):
-        at = pl.ds(pl.multiple_of(k * tile, tile), tile)
+    def work(k):
+        at = pl.ds(k * tile if first else pl.multiple_of(k * tile, tile), tile)
+        have = train
+        if first and k * tile >= early:
+            have = more_train
+            if k * tile == early:
+                copy.wait()
         left, right = [], []
         for dy, dz, parts in plan:
             left.append(jnp.concatenate([piece(part, 0, half) for part in parts], axis=0))
             block = ((y + dy) % SIDE) * SIDE + (z + dz) % SIDE
-            right.append(train[at, pl.ds(pl.multiple_of(block * 128, 128), 128)])
+            right.append(have[at, pl.ds(pl.multiple_of(block * 128, 128), 128)])
         if first:
             left.append(label_rows[to, :])
             right.append(train_hot[at, :])
@@ -194,10 +208,16 @@
             out[:, at] = peak + jnp.log2(total)
         scores[to, at] = x
 
-
-def product_part(name, plan, row, tile, train, given, alpha=None):
+    if first:
+        for k in range(rows // tile):
+            work(k)
+    else:
+        pl.loop(0, rows // tile, unroll=not last)(work)
+
+
+def product_part(name, plan, row, tile, train, given, alpha=None, source=None, early=None):
     rows = train.shape[0]
-    first, last = given[0].dtype == jnp.bfloat16, alpha is not None
+    first, last = source is not None, alpha is not None
     cols = given[0].shape[0]
     vals = []
 
@@ -213,15 +233,22 @@
     out.append(shape_of((1, rows)) if last else shape_of((cols, 128)))
     given = given if first else [in_vmem(given[0]), given[1]]
     operands = [*vals, in_vmem(train), *given]
+    specs = [VMEM] * len(operands)
+    scratch, aliases = [], {len(operands) - 2: 0}
+    if first:
+        out.append(pltpu.VMEM(train.shape, train.dtype))
+        operands.append(in_hbm(source))
+        specs.append(HBM)
+        scratch, aliases = [pltpu.SemaphoreType.DMA], {len(vals): 2}
     depth = len(plan) * 128
     height = len(plan[0][2]) * cols // 2
     return pl.pallas_call(
-        lambda *refs: part_kernel(plan, len(vals), row, tile, alpha, *refs),
+        lambda *refs: part_kernel(plan, len(vals), row, tile, alpha, early, *refs),
         out_shape=tuple(out),
-        in_specs=[VMEM] * len(operands),
+        in_specs=specs,
         out_specs=(VMEM,) * len(out),
-        scratch_shapes=[pltpu.VMEM((height, 128), jnp.float32)] if last else [],
-        input_output_aliases={} if first else {len(operands) - 2: 0},
+        scratch_shapes=[pltpu.VMEM((height, 128), jnp.float32)] if last else scratch,
+        input_output_aliases=aliases,
         compiler_params=params(SMALL),
         cost_estimate=pl.CostEstimate(
             flops=2 * height * rows * depth, bytes_accessed=0, transcendentals=0
@@ -325,12 +352,19 @@
     sums[...] = jnp.sum(out, axis=0, keepdims=True)
 
 
-def cols_kernel(total_cols, kern, weights, r0, r1, r2, r3, sums):
-    u = total_cols / ((r0[...] + r1[...]) + (r2[...] + r3[...]))
-    out = lax.dot_general(split_rows(u), kern[...], LAST, preferred_element_type=jnp.float32)
-    out = jnp.sum(out, axis=0, keepdims=True) * weights[...]
-    for g in range(sums.shape[0]):
-        sums[g] = out
+def cols_kernel(total_cols, kern, weights, r0, r1, r2, r3, sums, u):
+    cols, rows = kern.shape
+    u[...] = total_cols / ((r0[...] + r1[...]) + (r2[...] + r3[...]))
+    block = 256
+    for k in range(0, cols, block):
+        part = pl.ds(k, block)
+        total = jnp.zeros((block, 128), jnp.float32)
+        for c in range(rows // 128):
+            lane = pl.ds(c * 128, 128)
+            total = total + kern[part, lane].astype(jnp.float32) * u[:, lane]
+        out = lane_sums(total) * weights[:, part]
+        for g in range(sums.shape[0]):
+            sums[g, :, part] = out
 
 
 def other_chips(x):
@@ -357,6 +391,7 @@
     vec_r, vec_c = shape_of((1, rows)), shape_of((1, cols))
 
     near, diagonal, last_a, last_b = gather(val_embed)
+    early = rows // 3072 * 2048
     train, train_hot, label_rows = pl.pallas_call(
         lambda *refs: prepare_kernel(features, 512, *refs),
         out_shape=(
@@ -370,7 +405,7 @@
             pltpu.VMEM((1, rows), jnp.int32),
             pltpu.VMEM((1, cols), jnp.int32),
             pltpu.VMEM(label_cost.shape, jnp.float32),
-            pltpu.SemaphoreType.DMA((rows // 512,)),
+            pltpu.SemaphoreType.DMA((early // 512,)),
             pltpu.SemaphoreType.DMA((3,)),
         ],
         compiler_params=params(SMALL),
@@ -382,7 +417,16 @@
         in_hbm(train_embed),
     )
     alpha = 2.0 * KAPPA / features
-    given = product_part("product_near", near, 0, 1024, train, [label_rows, train_hot])
+    *given, train = product_part(
+        "product_near",
+        near,
+        0,
+        1024,
+        train,
+        [label_rows, train_hot],
+        source=train_embed,
+        early=early,
+    )
     scores, squares = product_part("product_diagonal", diagonal, 0, 1024, train, given)
     scores, log_a = product_part("product_a", last_a, 0, 1536, train, [scores, squares], alpha)
     scores, log_b = product_part(
@@ -418,6 +462,7 @@
             out_shape=shape_of((groups, 1, cols)),
             in_specs=[VMEM] * 6,
             out_specs=VMEM,
+            scratch_shapes=[pltpu.VMEM((1, rows), jnp.float32)],
             compiler_params=params(SMALL),
             name="columns",
         )(kern, weights, both, *others)

time: 121 us -> 121 us (level)
  Pallas kernels: 41.3 us -> 40 us
    pallas_call x1, Pallas kernels: 4.79 us -> 3.57 us  [shards(): pl.pallas_call(lambda *refs: prepare_kernel(features, 512, *refs), out_sh...]
  transfers between devices with their start and end apart: 26 -> 26, of which waited for: 14 -> 13; matrix products, arithmetic and copies ran while one was open for 0% -> 0% of each run, Pallas kernels for 23% -> 22%
where the time goes in v2:
time: 121 us; the launch traced here: 120 us
  starting transfers between devices  40 us (33%)
  Pallas kernels  40 us (33%)
  blocking collectives  24 us (20%)
  waiting for transfers between devices  14.5 us (12%)
    all_to_all x2, blocking collectives, spread(): return lax.all_to_all(x, 'train', 0, 0)  24 us
    ppermute x13, starting transfers between devices, from_step(): return lax.ppermute(x, 'train', pairs)  22.1 us
    pallas_call x4, Pallas kernels, product_part(): pl.pallas_call(lambda *refs: part_kernel(plan, len(vals), row, tile, alph...  21 us
    ppermute x9, starting transfers between devices, other_chips(): lax.ppermute(x, 'val', [(i, (i + 2 * k) % n) for i in range(n)])  14.1 us
    ppermute x9, waiting for transfers between devices, other_chips(): lax.ppermute(x, 'val', [(i, (i + 2 * k) % n) for i in range(n)])  8.19 us
    pallas_call x1, Pallas kernels, shards(): pl.pallas_call(lambda *refs: train_kernel(256, math.log2(total_cols), *re...  6.37 us
    pallas_call x2, Pallas kernels, shards(): pl.pallas_call(lambda *refs: cols_kernel(total_cols, *refs), out_shape=sh...  3.82 us
    pallas_call x1, Pallas kernels, shards(): pl.pallas_call(lambda *refs: prepare_kernel(features, 512, *refs), out_sh...  3.57 us
  transfers between devices with their start and end apart: 26, of which 13 were waited for; matrix products, arithmetic and copies ran while one was open for 0% of the time, Pallas kernels for 22%

profile of v2, /device:TPU:0, one launch (start us, length us, event | category | flops | bytes accessed | tf_op | source)
XLA Modules:
  0.0 120.5 jit_solution(9134817825057015372)
XLA Ops:
  0.6 3.2 %collective-permute-start.1 = (bf16[1024,128]{1,0:T(8,128)(2,1)}, bf16[1024,128]{1,0:T(8,128)(2,1)S(1)}, u32[]{:S(2)}, u32[]{:S(2)}) collective-permute-start(bf16[1024,128]{1,0:T(8,128)(2,1)} %refs_0_.4), channel_id=1, source_target_pairs={{0,96},{8,104},{16,112},{24,120},{32,0},{40,8},{48,16},{56,24},{64... | collective-permute-start | bytes 786440 | tf_op jit(solution)/shard_map/ppermute | solution.py:266
  3.8 1.9 %collective-permute-start = (bf16[1024,128]{1,0:T(8,128)(2,1)}, bf16[1024,128]{1,0:T(8,128)(2,1)S(1)}, u32[]{:S(2)}, u32[]{:S(2)}) collective-permute-start(bf16[1024,128]{1,0:T(8,128)(2,1)} %refs_0_.4), channel_id=1, source_target_pairs={{0,8},{8,16},{16,24},{24,0},{32,40},{40,48},{48,56},{56,32},{64,72... | collective-permute-start | bytes 786440 | tf_op jit(solution)/shard_map/ppermute | solution.py:266
  5.7 2.1 %collective-permute-start.7 = (bf16[1024,128]{1,0:T(8,128)(2,1)}, bf16[1024,128]{1,0:T(8,128)(2,1)S(1)}, u32[]{:S(2)}, u32[]{:S(2)}) collective-permute-start(bf16[1024,128]{1,0:T(8,128)(2,1)} %refs_0_.4), channel_id=1, source_target_pairs={{0,24},{8,0},{16,8},{24,16},{32,56},{40,32},{48,40},{56,48},{64,88... | collective-permute-start | bytes 786440 | tf_op jit(solution)/shard_map/ppermute | solution.py:266
  7.9 3.6 %prepare.1 = (bf16[3072,2048]{1,0:T(8,128)(2,1)S(1)}, bf16[3072,128]{1,0:T(8,128)(2,1)S(1)}, bf16[1024,128]{1,0:T(8,128)(2,1)S(1)}) custom-call(f32[10,10]{1,0:T(8,128)} %refs_0_.3, s32[1,3072]{1,0:T(1,128)} %bitcast.6, s32[1,1024]{1,0:T(1,128)} %bitcast.8, bf16[3072,2048]{1,0:T(8,128)(2,1)} %refs_0_.5), custom_call_target="tpu_custom_call" | custom-call | tf_op jit(solution)/shard_map/prepare/pallas_call | solution.py:395
  13.0 2.0 %collective-permute-start.3 = (bf16[1024,128]{1,0:T(8,128)(2,1)S(1)}, bf16[1024,128]{1,0:T(8,128)(2,1)S(1)}, u32[]{:S(2)}, u32[]{:S(2)}) collective-permute-start(bf16[1024,128]{1,0:T(8,128)(2,1)S(1)} %pad_maximum_fusion.4), channel_id=1, source_target_pairs={{0,8},{8,16},{16,24},{24,0},{32,40},{40,48},{48,56},{56,32},{64,72... | collective-permute-start | bytes 786440 | tf_op jit(solution)/shard_map/ppermute | solution.py:266
  15.0 2.2 %collective-permute-start.5 = (bf16[1024,128]{1,0:T(8,128)(2,1)S(1)}, bf16[1024,128]{1,0:T(8,128)(2,1)S(1)}, u32[]{:S(2)}, u32[]{:S(2)}) collective-permute-start(bf16[1024,128]{1,0:T(8,128)(2,1)S(1)} %pad_maximum_fusion.4), channel_id=1, source_target_pairs={{0,24},{8,0},{16,8},{24,16},{32,56},{40,32},{48,40},{56,48},{64,88... | collective-permute-start | bytes 786440 | tf_op jit(solution)/shard_map/ppermute | solution.py:266
  17.4 3.2 %collective-permute-start.8 = (bf16[1024,128]{1,0:T(8,128)(2,1)S(1)}, bf16[1024,128]{1,0:T(8,128)(2,1)S(1)}, u32[]{:S(2)}, u32[]{:S(2)}) collective-permute-start(bf16[1024,128]{1,0:T(8,128)(2,1)S(1)} %pad_maximum_fusion.5), channel_id=1, source_target_pairs={{0,96},{8,104},{16,112},{24,120},{32,0},{40,8},{48,16},{56,24},{64... | collective-permute-start | bytes 786440 | tf_op jit(solution)/shard_map/ppermute | solution.py:266
  21.8 5.4 %product_near.1 = (f32[1024,3072]{1,0:T(8,128)S(1)}, f32[1024,128]{1,0:T(8,128)S(1)}, bf16[3072,2048]{1,0:T(8,128)(2,1)S(1)}) custom-call(bf16[1024,128]{1,0:T(8,128)(2,1)S(1)} %copy-done, bf16[1024,128]{1,0:T(8,128)(2,1)S(1)} %collective-permute-done.7.refs_1_, bf16[1024,128]{1,0:T(8,128)(2,1)S(1)} %collective-permute-done.refs_2_, ...), custom_call_target="tpu_custom_call", output_to_operand_aliasing={{2}: (5, {})} | custom-call | flops 4026531840 | tf_op jit(solution)/shard_map/product_near/pallas_call | solution.py:245
  27.3 1.7 %collective-permute-start.10 = (bf16[1536,128]{1,0:T(8,128)(2,1)S(1)}, bf16[1536,128]{1,0:T(8,128)(2,1)S(1)}, u32[]{:S(2)}, u32[]{:S(2)}) collective-permute-start(bf16[1536,128]{1,0:T(8,128)(2,1)S(1)} %pad_maximum_fusion.2), channel_id=1, source_target_pairs={{0,24},{8,0},{16,8},{24,16},{32,56},{40,32},{48,40},{56,48},{64,88... | collective-permute-start | bytes 1179656 | tf_op jit(solution)/shard_map/ppermute | solution.py:266
  30.3 2.7 %collective-permute-start.6 = (bf16[1536,128]{1,0:T(8,128)(2,1)S(1)}, bf16[1536,128]{1,0:T(8,128)(2,1)S(1)}, u32[]{:S(2)}, u32[]{:S(2)}) collective-permute-start(bf16[1536,128]{1,0:T(8,128)(2,1)S(1)} %pad_maximum_fusion.1), channel_id=1, source_target_pairs={{0,96},{8,104},{16,112},{24,120},{32,0},{40,8},{48,16},{56,24},{64... | collective-permute-start | bytes 1179656 | tf_op jit(solution)/shard_map/ppermute | solution.py:266
  33.6 6.3 %product_diagonal.1 = (f32[1024,3072]{1,0:T(8,128)S(1)}, f32[1024,128]{1,0:T(8,128)S(1)}) custom-call(bf16[1024,128]{1,0:T(8,128)(2,1)S(1)} %collective-permute-done.8.refs_0_, bf16[1024,128]{1,0:T(8,128)(2,1)S(1)} %collective-permute-done.5.refs_1_, bf16[1024,128]{1,0:T(8,128)(2,1)S(1)} %collective-permute-done.3.refs_2_, ...), custom_call_target="tpu_custom_call", output_to_operand_aliasing={{0}: (6, {})} | custom-call | flops 4026531840 | tf_op jit(solution)/shard_map/product_diagonal/pallas_call | solution.py:245
  40.0 4.6 %product_a.1 = (f32[1024,3072]{1,0:T(8,128)S(1)}, f32[1,3072]{1,0:T(1,128)S(1)}) custom-call(bf16[1536,128]{1,0:T(8,128)(2,1)S(1)} %collective-permute-done.10.refs_0_, bf16[1536,128]{1,0:T(8,128)(2,1)S(1)} %collective-permute-done.11.refs_1_, bf16[3072,2048]{1,0:T(8,128)(2,1)S(1)} %get-tuple-element.24.refs_5_.refs_2_, ...), custom_call_target="tpu_custom_call", output_to_operand_aliasing={{0}: (3, {})} | custom-call | flops 2415919104 | tf_op jit(solution)/shard_map/product_a/pallas_call | solution.py:245
  44.7 4.6 %product_b.1 = (f32[1024,3072]{1,0:T(8,128)S(1)}, f32[1,3072]{1,0:T(1,128)S(1)}) custom-call(bf16[1536,128]{1,0:T(8,128)(2,1)S(1)} %collective-permute-done.4.refs_0_, bf16[1536,128]{1,0:T(8,128)(2,1)S(1)} %collective-permute-done.6.refs_1_, bf16[3072,2048]{1,0:T(8,128)(2,1)S(1)} %get-tuple-element.24.refs_5_.refs_2_, ...), custom_call_target="tpu_custom_call", output_to_operand_aliasing={{0}: (3, {})} | custom-call | flops 2415919104 | tf_op jit(solution)/shard_map/product_b/pallas_call | solution.py:245
  52.3 2.8 %collective-permute-start.15 = (f32[1,3072]{1,0:T(1,128)S(1)}, f32[1,3072]{1,0:T(1,128)S(1)}, u32[]{:S(2)}, u32[]{:S(2)}) collective-permute-start(f32[1,3072]{1,0:T(1,128)S(1)} %compare_select_fusion.refs_1_), channel_id=1, source_target_pairs={{0,4},{1,5},{2,6},{3,7},{4,0},{5,1},{6,2},{7,3},{8,12},{9,13},{10,... | collective-permute-start | bytes 36872 | tf_op jit(solution)/shard_map/ppermute | solution.py:373
  58.7 3.2 %kernel_matrix.1 = (bf16[1024,3072]{1,0:T(8,128)(2,1)S(1)}, f32[1,3072]{1,0:T(1,128)S(1)}, f32[1,1024]{1,0:T(1,128)S(1)}, f32[16,1,1024]{2,1,0:T(1,128)S(1)}) custom-call(f32[1024,3072]{1,0:T(8,128)S(1)} %get-tuple-element.30.refs_0_, f32[1,3072]{1,0:T(1,128)S(1)} %compare_select_fusion.refs_1_, f32[1,3072]{1,0:T(1,128)S(1)} %collective-permute-done.14.refs_2_, ...), custom_call_target="tpu_custom_call" | custom-call | tf_op jit(solution)/shard_map/kernel_matrix/pallas_call | solution.py:438
  62.0 13.1 %all_to_all.15.refs_2_ = f32[16,1,1024]{2,1,0:T(1,128)S(1)} all-to-all(f32[16,1,1024]{2,1,0:T(1,128)S(1)} %get-tuple-element.36), channel_id=1, replica_groups=mesh['train'=16,'val'=8] {'train'}, dimensions={0} | all-to-all | bytes 131072 | tf_op jit(solution)/shard_map/all_to_all | solution.py:382
  77.7 3.8 %collective-permute-start.19 = (f32[1,3072]{1,0:T(1,128)S(1)}, f32[1,3072]{1,0:T(1,128)S(1)}, u32[]{:S(2)}, u32[]{:S(2)}) collective-permute-start(f32[1,3072]{1,0:T(1,128)S(1)} %add.22.refs_2_), channel_id=1, source_target_pairs={{0,4},{1,5},{2,6},{3,7},{4,0},{5,1},{6,2},{7,3},{8,12},{9,13},{10,... | collective-permute-start | bytes 36872 | tf_op jit(solution)/shard_map/ppermute | solution.py:373
  83.3 1.9 %collective-permute-done.20.refs_5_ = f32[1,3072]{1,0:T(1,128)S(1)} collective-permute-done((f32[1,3072]{1,0:T(1,128)S(1)}, f32[1,3072]{1,0:T(1,128)S(1)}, u32[]{:S(2)}, u32[]{:S(2)}) %collective-permute-start.20) | collective-permute-done | bytes 12320 | tf_op jit(solution)/shard_map/ppermute | solution.py:373
  85.2 1.6 %columns.2 = f32[16,1,1024]{2,1,0:T(1,128)S(1)} custom-call(bf16[1024,3072]{1,0:T(8,128)(2,1)S(1)} %get-tuple-element.34.refs_0_, f32[1,1024]{1,0:T(1,128)S(1)} %get-tuple-element.37.refs_1_, f32[1,3072]{1,0:T(1,128)S(1)} %add.22.refs_2_, f32[1,3072]{1,0:T(1,128)S(1)} %collective-permute-done.18.refs_3_, f32[1,3072]{1,0:T(1,128)S(1)} %collective-permute-done.19.refs_4_, ...), custom_call_target="tpu_custom_call" | custom-call | tf_op jit(solution)/shard_map/columns/pallas_call | solution.py:460
  86.8 10.9 %all_to_all.16.refs_2_ = f32[16,1,1024]{2,1,0:T(1,128)S(1)} all-to-all(f32[16,1,1024]{2,1,0:T(1,128)S(1)} %columns.2), channel_id=1, replica_groups=mesh['train'=16,'val'=8] {'train'}, dimensions={0} | all-to-all | bytes 131072 | tf_op jit(solution)/shard_map/all_to_all | solution.py:382
  100.1 2.7 %collective-permute-start.23 = (f32[1,3072]{1,0:T(1,128)S(1)}, f32[1,3072]{1,0:T(1,128)S(1)}, u32[]{:S(2)}, u32[]{:S(2)}) collective-permute-start(f32[1,3072]{1,0:T(1,128)S(1)} %add.23.refs_2_), channel_id=1, source_target_pairs={{0,4},{1,5},{2,6},{3,7},{4,0},{5,1},{6,2},{7,3},{8,12},{9,13},{10,... | collective-permute-start | bytes 36872 | tf_op jit(solution)/shard_map/ppermute | solution.py:373
  106.5 2.2 %columns.3 = f32[16,1,1024]{2,1,0:T(1,128)} custom-call(bf16[1024,3072]{1,0:T(8,128)(2,1)S(1)} %get-tuple-element.34.refs_0_, f32[1,1024]{1,0:T(1,128)S(1)} %get-tuple-element.37.refs_1_, f32[1,3072]{1,0:T(1,128)S(1)} %add.23.refs_2_, f32[1,3072]{1,0:T(1,128)S(1)} %collective-permute-done.22.refs_3_, f32[1,3072]{1,0:T(1,128)S(1)} %collective-permute-done.23.refs_4_, ...), custom_call_target="tpu_custom_call" | custom-call | tf_op jit(solution)/shard_map/columns/pallas_call | solution.py:460
  108.7 3.5 %all-to-all-start.2 = ((f32[16,1,1024]{2,1,0:T(1,128)}), f32[16,1,1024]{2,1,0:T(1,128)S(1)}, u32[]{:S(2)}, u32[]{:S(2)}) async-start(f32[16,1,1024]{2,1,0:T(1,128)} %columns.3), calls=%async_computation.2 | async-start | bytes 131072 | tf_op jit(solution)/shard_map/all_to_all | solution.py:382
  112.2 6.4 %train_potential.1 = f32[1,3072]{1,0:T(1,128)} custom-call(bf16[3072,2048]{1,0:T(8,128)(2,1)} %refs_0_.5, f32[1,3072]{1,0:T(1,128)S(1)} %get-tuple-element.33.refs_1_, f32[1,3072]{1,0:T(1,128)S(1)} %add.23.refs_2_, f32[1,3072]{1,0:T(1,128)S(1)} %collective-permute-done.22.refs_3_, f32[1,3072]{1,0:T(1,128)S(1)} %collective-permute-done.23.refs_4_, ...), custom_call_target="tpu_custom_call" | custom-call | tf_op jit(solution)/shard_map/train_potential/pallas_call | solution.py:480
  (64 shorter events, 23.9 us)
Async XLA Ops:
  0.6 10.8 %collective-permute-start.1 = (bf16[1024,128]{1,0:T(8,128)(2,1)}, bf16[1024,128]{1,0:T(8,128)(2,1)S(1)}, u32[]{:S(2)}, u32[]{:S(2)}) collective-permute-start(bf16[1024,128]{1,0:T(8,128)(2,1)} %refs_0_.4), channel_id=1, source_target_pairs={{0,96},{8,104},{16,112},{24,120},{32,0},{40,8},{48,16},{56,24},{64... | collective-permute-start | bytes 786440 | tf_op jit(solution)/shard_map/ppermute | solution.py:266
  3.8 9.2 %collective-permute-start.2 = (bf16[1024,128]{1,0:T(8,128)(2,1)}, bf16[1024,128]{1,0:T(8,128)(2,1)S(1)}, u32[]{:S(2)}, u32[]{:S(2)}) collective-permute-start(bf16[1024,128]{1,0:T(8,128)(2,1)} %refs_0_.4), channel_id=1, source_target_pairs={{0,32},{8,40},{16,48},{24,56},{32,64},{40,72},{48,80},{56,88},{64,... | collective-permute-start | bytes 786440 | tf_op jit(solution)/shard_map/ppermute | solution.py:266
  3.8 13.4 %collective-permute-start = (bf16[1024,128]{1,0:T(8,128)(2,1)}, bf16[1024,128]{1,0:T(8,128)(2,1)S(1)}, u32[]{:S(2)}, u32[]{:S(2)}) collective-permute-start(bf16[1024,128]{1,0:T(8,128)(2,1)} %refs_0_.4), channel_id=1, source_target_pairs={{0,8},{8,16},{16,24},{24,0},{32,40},{40,48},{48,56},{56,32},{64,72... | collective-permute-start | bytes 786440 | tf_op jit(solution)/shard_map/ppermute | solution.py:266
  5.7 11.5 %collective-permute-start.7 = (bf16[1024,128]{1,0:T(8,128)(2,1)}, bf16[1024,128]{1,0:T(8,128)(2,1)S(1)}, u32[]{:S(2)}, u32[]{:S(2)}) collective-permute-start(bf16[1024,128]{1,0:T(8,128)(2,1)} %refs_0_.4), channel_id=1, source_target_pairs={{0,24},{8,0},{16,8},{24,16},{32,56},{40,32},{48,40},{56,48},{64,88... | collective-permute-start | bytes 786440 | tf_op jit(solution)/shard_map/ppermute | solution.py:266
  13.0 17.2 %collective-permute-start.3 = (bf16[1024,128]{1,0:T(8,128)(2,1)S(1)}, bf16[1024,128]{1,0:T(8,128)(2,1)S(1)}, u32[]{:S(2)}, u32[]{:S(2)}) collective-permute-start(bf16[1024,128]{1,0:T(8,128)(2,1)S(1)} %pad_maximum_fusion.4), channel_id=1, source_target_pairs={{0,8},{8,16},{16,24},{24,0},{32,40},{40,48},{48,56},{56,32},{64,72... | collective-permute-start | bytes 786440 | tf_op jit(solution)/shard_map/ppermute | solution.py:266
  15.0 15.2 %collective-permute-start.5 = (bf16[1024,128]{1,0:T(8,128)(2,1)S(1)}, bf16[1024,128]{1,0:T(8,128)(2,1)S(1)}, u32[]{:S(2)}, u32[]{:S(2)}) collective-permute-start(bf16[1024,128]{1,0:T(8,128)(2,1)S(1)} %pad_maximum_fusion.4), channel_id=1, source_target_pairs={{0,24},{8,0},{16,8},{24,16},{32,56},{40,32},{48,40},{56,48},{64,88... | collective-permute-start | bytes 786440 | tf_op jit(solution)/shard_map/ppermute | solution.py:266
  17.3 9.9 %collective-permute-start.9 = (bf16[1024,128]{1,0:T(8,128)(2,1)S(1)}, bf16[1024,128]{1,0:T(8,128)(2,1)S(1)}, u32[]{:S(2)}, u32[]{:S(2)}) collective-permute-start(bf16[1024,128]{1,0:T(8,128)(2,1)S(1)} %pad_maximum_fusion.5), channel_id=1, source_target_pairs={{0,32},{8,40},{16,48},{24,56},{32,64},{40,72},{48,80},{56,88},{64,... | collective-permute-start | bytes 786440 | tf_op jit(solution)/shard_map/ppermute | solution.py:266
  17.4 9.9 %collective-permute-start.8 = (bf16[1024,128]{1,0:T(8,128)(2,1)S(1)}, bf16[1024,128]{1,0:T(8,128)(2,1)S(1)}, u32[]{:S(2)}, u32[]{:S(2)}) collective-permute-start(bf16[1024,128]{1,0:T(8,128)(2,1)S(1)} %pad_maximum_fusion.5), channel_id=1, source_target_pairs={{0,96},{8,104},{16,112},{24,120},{32,0},{40,8},{48,16},{56,24},{64... | collective-permute-start | bytes 786440 | tf_op jit(solution)/shard_map/ppermute | solution.py:266
  20.6 13.0 %collective-permute-start.12 = (bf16[1024,128]{1,0:T(8,128)(2,1)S(1)}, bf16[1024,128]{1,0:T(8,128)(2,1)S(1)}, u32[]{:S(2)}, u32[]{:S(2)}) collective-permute-start(bf16[1024,128]{1,0:T(8,128)(2,1)S(1)} %collective-permute-done.1.refs_3_), channel_id=1, source_target_pairs={{0,112},{8,120},{16,96},{24,104},{32,16},{40,24},{48,0},{56,8},{64... | collective-permute-start | bytes 786440 | tf_op jit(solution)/shard_map/ppermute | solution.py:266
  27.3 12.6 %collective-permute-start.10 = (bf16[1536,128]{1,0:T(8,128)(2,1)S(1)}, bf16[1536,128]{1,0:T(8,128)(2,1)S(1)}, u32[]{:S(2)}, u32[]{:S(2)}) collective-permute-start(bf16[1536,128]{1,0:T(8,128)(2,1)S(1)} %pad_maximum_fusion.2), channel_id=1, source_target_pairs={{0,24},{8,0},{16,8},{24,16},{32,56},{40,32},{48,40},{56,48},{64,88... | collective-permute-start | bytes 1179656 | tf_op jit(solution)/shard_map/ppermute | solution.py:266
  29.1 10.9 %collective-permute-start.11 = (bf16[1536,128]{1,0:T(8,128)(2,1)S(1)}, bf16[1536,128]{1,0:T(8,128)(2,1)S(1)}, u32[]{:S(2)}, u32[]{:S(2)}) collective-permute-start(bf16[1536,128]{1,0:T(8,128)(2,1)S(1)} %pad_maximum_fusion.3), channel_id=1, source_target_pairs={{0,32},{8,40},{16,48},{24,56},{32,64},{40,72},{48,80},{56,88},{64,... | collective-permute-start | bytes 1179656 | tf_op jit(solution)/shard_map/ppermute | solution.py:266
  30.3 14.3 %collective-permute-start.6 = (bf16[1536,128]{1,0:T(8,128)(2,1)S(1)}, bf16[1536,128]{1,0:T(8,128)(2,1)S(1)}, u32[]{:S(2)}, u32[]{:S(2)}) collective-permute-start(bf16[1536,128]{1,0:T(8,128)(2,1)S(1)} %pad_maximum_fusion.1), channel_id=1, source_target_pairs={{0,96},{8,104},{16,112},{24,120},{32,0},{40,8},{48,16},{56,24},{64... | collective-permute-start | bytes 1179656 | tf_op jit(solution)/shard_map/ppermute | solution.py:266
  33.0 11.6 %collective-permute-start.4 = (bf16[1536,128]{1,0:T(8,128)(2,1)S(1)}, bf16[1536,128]{1,0:T(8,128)(2,1)S(1)}, u32[]{:S(2)}, u32[]{:S(2)}) collective-permute-start(bf16[1536,128]{1,0:T(8,128)(2,1)S(1)} %pad_maximum_fusion), channel_id=1, source_target_pairs={{0,8},{8,16},{16,24},{24,0},{32,40},{40,48},{48,56},{56,32},{64,72... | collective-permute-start | bytes 1179656 | tf_op jit(solution)/shard_map/ppermute | solution.py:266
  49.4 1.3 %collective-permute-start.13 = (f32[1,3072]{1,0:T(1,128)S(1)}, f32[1,3072]{1,0:T(1,128)S(1)}, u32[]{:S(2)}, u32[]{:S(2)}) collective-permute-start(f32[1,3072]{1,0:T(1,128)S(1)} %compare_select_fusion.1), channel_id=1, source_target_pairs={{0,1},{1,0},{2,3},{3,2},{4,5},{5,4},{6,7},{7,6},{8,9},{9,8},{10,11... | collective-permute-start | bytes 36872 | tf_op jit(solution)/shard_map/ppermute | solution.py:378
  50.7 5.7 %collective-permute-start.14 = (f32[1,3072]{1,0:T(1,128)S(1)}, f32[1,3072]{1,0:T(1,128)S(1)}, u32[]{:S(2)}, u32[]{:S(2)}) collective-permute-start(f32[1,3072]{1,0:T(1,128)S(1)} %compare_select_fusion.refs_1_), channel_id=1, source_target_pairs={{0,2},{1,3},{2,4},{3,5},{4,6},{5,7},{6,0},{7,1},{8,10},{9,11},{10,... | collective-permute-start | bytes 36872 | tf_op jit(solution)/shard_map/ppermute | solution.py:373
  52.3 5.2 %collective-permute-start.15 = (f32[1,3072]{1,0:T(1,128)S(1)}, f32[1,3072]{1,0:T(1,128)S(1)}, u32[]{:S(2)}, u32[]{:S(2)}) collective-permute-start(f32[1,3072]{1,0:T(1,128)S(1)} %compare_select_fusion.refs_1_), channel_id=1, source_target_pairs={{0,4},{1,5},{2,6},{3,7},{4,0},{5,1},{6,2},{7,3},{8,12},{9,13},{10,... | collective-permute-start | bytes 36872 | tf_op jit(solution)/shard_map/ppermute | solution.py:373
  55.0 3.7 %collective-permute-start.16 = (f32[1,3072]{1,0:T(1,128)S(1)}, f32[1,3072]{1,0:T(1,128)S(1)}, u32[]{:S(2)}, u32[]{:S(2)}) collective-permute-start(f32[1,3072]{1,0:T(1,128)S(1)} %compare_select_fusion.refs_1_), channel_id=1, source_target_pairs={{0,6},{1,7},{2,0},{3,1},{4,2},{5,3},{6,4},{7,5},{8,14},{9,15},{10,... | collective-permute-start | bytes 36872 | tf_op jit(solution)/shard_map/ppermute | solution.py:373
  77.3 5.0 %collective-permute-start.18 = (f32[1,3072]{1,0:T(1,128)S(1)}, f32[1,3072]{1,0:T(1,128)S(1)}, u32[]{:S(2)}, u32[]{:S(2)}) collective-permute-start(f32[1,3072]{1,0:T(1,128)S(1)} %add.22.refs_2_), channel_id=1, source_target_pairs={{0,2},{1,3},{2,4},{3,5},{4,6},{5,7},{6,0},{7,1},{8,10},{9,11},{10,... | collective-permute-start | bytes 36872 | tf_op jit(solution)/shard_map/ppermute | solution.py:373
  77.7 5.6 %collective-permute-start.19 = (f32[1,3072]{1,0:T(1,128)S(1)}, f32[1,3072]{1,0:T(1,128)S(1)}, u32[]{:S(2)}, u32[]{:S(2)}) collective-permute-start(f32[1,3072]{1,0:T(1,128)S(1)} %add.22.refs_2_), channel_id=1, source_target_pairs={{0,4},{1,5},{2,6},{3,7},{4,0},{5,1},{6,2},{7,3},{8,12},{9,13},{10,... | collective-permute-start | bytes 36872 | tf_op jit(solution)/shard_map/ppermute | solution.py:373
  81.5 3.7 %collective-permute-start.20 = (f32[1,3072]{1,0:T(1,128)S(1)}, f32[1,3072]{1,0:T(1,128)S(1)}, u32[]{:S(2)}, u32[]{:S(2)}) collective-permute-start(f32[1,3072]{1,0:T(1,128)S(1)} %add.22.refs_2_), channel_id=1, source_target_pairs={{0,6},{1,7},{2,0},{3,1},{4,2},{5,3},{6,4},{7,5},{8,14},{9,15},{10,... | collective-permute-start | bytes 36872 | tf_op jit(solution)/shard_map/ppermute | solution.py:373
  100.0 5.0 %collective-permute-start.22 = (f32[1,3072]{1,0:T(1,128)S(1)}, f32[1,3072]{1,0:T(1,128)S(1)}, u32[]{:S(2)}, u32[]{:S(2)}) collective-permute-start(f32[1,3072]{1,0:T(1,128)S(1)} %add.23.refs_2_), channel_id=1, source_target_pairs={{0,2},{1,3},{2,4},{3,5},{4,6},{5,7},{6,0},{7,1},{8,10},{9,11},{10,... | collective-permute-start | bytes 36872 | tf_op jit(solution)/shard_map/ppermute | solution.py:373
  100.1 5.3 %collective-permute-start.23 = (f32[1,3072]{1,0:T(1,128)S(1)}, f32[1,3072]{1,0:T(1,128)S(1)}, u32[]{:S(2)}, u32[]{:S(2)}) collective-permute-start(f32[1,3072]{1,0:T(1,128)S(1)} %add.23.refs_2_), channel_id=1, source_target_pairs={{0,4},{1,5},{2,6},{3,7},{4,0},{5,1},{6,2},{7,3},{8,12},{9,13},{10,... | collective-permute-start | bytes 36872 | tf_op jit(solution)/shard_map/ppermute | solution.py:373
  102.8 3.7 %collective-permute-start.24 = (f32[1,3072]{1,0:T(1,128)S(1)}, f32[1,3072]{1,0:T(1,128)S(1)}, u32[]{:S(2)}, u32[]{:S(2)}) collective-permute-start(f32[1,3072]{1,0:T(1,128)S(1)} %add.23.refs_2_), channel_id=1, source_target_pairs={{0,6},{1,7},{2,0},{3,1},{4,2},{5,3},{6,4},{7,5},{8,14},{9,15},{10,... | collective-permute-start | bytes 36872 | tf_op jit(solution)/shard_map/ppermute | solution.py:373
  108.7 11.1 %all-to-all-start.2 = ((f32[16,1,1024]{2,1,0:T(1,128)}), f32[16,1,1024]{2,1,0:T(1,128)S(1)}, u32[]{:S(2)}, u32[]{:S(2)}) async-start(f32[16,1,1024]{2,1,0:T(1,128)} %columns.3), calls=%async_computation.2 | async-start | bytes 131072 | tf_op jit(solution)/shard_map/all_to_all | solution.py:382
  (3 other events, 23.7 us)

commit v3 on v2

--- a/solution.py
+++ b/solution.py
@@ -272,7 +272,7 @@
     cut = lambda v, n: v[n * h : (n + 1) * h]
     z1, z3 = from_step(x, 0, 1), from_step(x, 0, 3)
     y1, y3 = from_step(x, 1, 0), from_step(x, 3, 0)
-    far = from_step(y1, 1, 2)
+    far = from_step(y3, 3, 2)
     both = lambda v: [low(v, 0), low(v, 1)]
     near = [(0, 0, both(x)), (0, 1, both(z1)), (0, 3, both(z3)), (1, 0, both(y1)), (3, 0, both(y3))]
 

time: 121 us -> 120 us (level)
  transfers between devices with their start and end apart: 26 -> 26, of which waited for: 13 -> 14; matrix products, arithmetic and copies ran while one was open for 0% -> 0% of each run, Pallas kernels for 22% -> 22%
where the time goes in v3:
time: 120 us; the launch traced here: 119 us
  Pallas kernels  40.1 us (33%)
  starting transfers between devices  38.8 us (32%)
  blocking collectives  23 us (19%)
  waiting for transfers between devices  15.5 us (13%)
    all_to_all x2, blocking collectives, spread(): return lax.all_to_all(x, 'train', 0, 0)  23 us
    pallas_call x4, Pallas kernels, product_part(): pl.pallas_call(lambda *refs: part_kernel(plan, len(vals), row, tile, alph...  21 us
    ppermute x13, starting transfers between devices, from_step(): return lax.ppermute(x, 'train', pairs)  21 us
    ppermute x9, starting transfers between devices, other_chips(): lax.ppermute(x, 'val', [(i, (i + 2 * k) % n) for i in range(n)])  14.1 us
    ppermute x9, waiting for transfers between devices, other_chips(): lax.ppermute(x, 'val', [(i, (i + 2 * k) % n) for i in range(n)])  8.17 us
    pallas_call x1, Pallas kernels, shards(): pl.pallas_call(lambda *refs: train_kernel(256, math.log2(total_cols), *re...  6.37 us
    pallas_call x2, Pallas kernels, shards(): pl.pallas_call(lambda *refs: cols_kernel(total_cols, *refs), out_shape=sh...  3.82 us
    pallas_call x1, Pallas kernels, shards(): pl.pallas_call(lambda *refs: prepare_kernel(features, 512, *refs), out_sh...  3.57 us
  transfers between devices with their start and end apart: 26, of which 14 were waited for; matrix products, arithmetic and copies ran while one was open for 0% of the time, Pallas kernels for 22%

profile of v3, /device:TPU:0, one launch (start us, length us, event | category | flops | bytes accessed | tf_op | source)
XLA Modules:
  0.0 119.5 jit_solution(12190182818793715325)
XLA Ops:
  0.6 3.2 %collective-permute-start.1 = (bf16[1024,128]{1,0:T(8,128)(2,1)}, bf16[1024,128]{1,0:T(8,128)(2,1)S(1)}, u32[]{:S(2)}, u32[]{:S(2)}) collective-permute-start(bf16[1024,128]{1,0:T(8,128)(2,1)} %refs_0_.4), channel_id=1, source_target_pairs={{0,96},{8,104},{16,112},{24,120},{32,0},{40,8},{48,16},{56,24},{64... | collective-permute-start | bytes 786440 | tf_op jit(solution)/shard_map/ppermute | solution.py:266
  3.8 1.9 %collective-permute-start = (bf16[1024,128]{1,0:T(8,128)(2,1)}, bf16[1024,128]{1,0:T(8,128)(2,1)S(1)}, u32[]{:S(2)}, u32[]{:S(2)}) collective-permute-start(bf16[1024,128]{1,0:T(8,128)(2,1)} %refs_0_.4), channel_id=1, source_target_pairs={{0,8},{8,16},{16,24},{24,0},{32,40},{40,48},{48,56},{56,32},{64,72... | collective-permute-start | bytes 786440 | tf_op jit(solution)/shard_map/ppermute | solution.py:266
  5.7 2.1 %collective-permute-start.7 = (bf16[1024,128]{1,0:T(8,128)(2,1)}, bf16[1024,128]{1,0:T(8,128)(2,1)S(1)}, u32[]{:S(2)}, u32[]{:S(2)}) collective-permute-start(bf16[1024,128]{1,0:T(8,128)(2,1)} %refs_0_.4), channel_id=1, source_target_pairs={{0,24},{8,0},{16,8},{24,16},{32,56},{40,32},{48,40},{56,48},{64,88... | collective-permute-start | bytes 786440 | tf_op jit(solution)/shard_map/ppermute | solution.py:266
  7.9 3.6 %prepare.1 = (bf16[3072,2048]{1,0:T(8,128)(2,1)S(1)}, bf16[3072,128]{1,0:T(8,128)(2,1)S(1)}, bf16[1024,128]{1,0:T(8,128)(2,1)S(1)}) custom-call(f32[10,10]{1,0:T(8,128)} %refs_0_.3, s32[1,3072]{1,0:T(1,128)} %bitcast.6, s32[1,1024]{1,0:T(1,128)} %bitcast.8, bf16[3072,2048]{1,0:T(8,128)(2,1)} %refs_0_.5), custom_call_target="tpu_custom_call" | custom-call | tf_op jit(solution)/shard_map/prepare/pallas_call | solution.py:395
  13.0 2.0 %collective-permute-start.3 = (bf16[1024,128]{1,0:T(8,128)(2,1)S(1)}, bf16[1024,128]{1,0:T(8,128)(2,1)S(1)}, u32[]{:S(2)}, u32[]{:S(2)}) collective-permute-start(bf16[1024,128]{1,0:T(8,128)(2,1)S(1)} %pad_maximum_fusion.4), channel_id=1, source_target_pairs={{0,8},{8,16},{16,24},{24,0},{32,40},{40,48},{48,56},{56,32},{64,72... | collective-permute-start | bytes 786440 | tf_op jit(solution)/shard_map/ppermute | solution.py:266
  15.0 2.2 %collective-permute-start.5 = (bf16[1024,128]{1,0:T(8,128)(2,1)S(1)}, bf16[1024,128]{1,0:T(8,128)(2,1)S(1)}, u32[]{:S(2)}, u32[]{:S(2)}) collective-permute-start(bf16[1024,128]{1,0:T(8,128)(2,1)S(1)} %pad_maximum_fusion.4), channel_id=1, source_target_pairs={{0,24},{8,0},{16,8},{24,16},{32,56},{40,32},{48,40},{56,48},{64,88... | collective-permute-start | bytes 786440 | tf_op jit(solution)/shard_map/ppermute | solution.py:266
  17.4 3.2 %collective-permute-start.8 = (bf16[1024,128]{1,0:T(8,128)(2,1)S(1)}, bf16[1024,128]{1,0:T(8,128)(2,1)S(1)}, u32[]{:S(2)}, u32[]{:S(2)}) collective-permute-start(bf16[1024,128]{1,0:T(8,128)(2,1)S(1)} %pad_maximum_fusion.5), channel_id=1, source_target_pairs={{0,96},{8,104},{16,112},{24,120},{32,0},{40,8},{48,16},{56,24},{64... | collective-permute-start | bytes 786440 | tf_op jit(solution)/shard_map/ppermute | solution.py:266
  20.7 5.4 %product_near.1 = (f32[1024,3072]{1,0:T(8,128)S(1)}, f32[1024,128]{1,0:T(8,128)S(1)}, bf16[3072,2048]{1,0:T(8,128)(2,1)S(1)}) custom-call(bf16[1024,128]{1,0:T(8,128)(2,1)S(1)} %copy-done, bf16[1024,128]{1,0:T(8,128)(2,1)S(1)} %collective-permute-done.7.refs_1_, bf16[1024,128]{1,0:T(8,128)(2,1)S(1)} %collective-permute-done.refs_2_, ...), custom_call_target="tpu_custom_call", output_to_operand_aliasing={{2}: (5, {})} | custom-call | flops 4026531840 | tf_op jit(solution)/shard_map/product_near/pallas_call | solution.py:245
  27.2 2.6 %collective-permute-start.10 = (bf16[1536,128]{1,0:T(8,128)(2,1)S(1)}, bf16[1536,128]{1,0:T(8,128)(2,1)S(1)}, u32[]{:S(2)}, u32[]{:S(2)}) collective-permute-start(bf16[1536,128]{1,0:T(8,128)(2,1)S(1)} %pad_maximum_fusion.2), channel_id=1, source_target_pairs={{0,24},{8,0},{16,8},{24,16},{32,56},{40,32},{48,40},{56,48},{64,88... | collective-permute-start | bytes 1179656 | tf_op jit(solution)/shard_map/ppermute | solution.py:266
  30.0 3.3 %collective-permute-start.6 = (bf16[1536,128]{1,0:T(8,128)(2,1)S(1)}, bf16[1536,128]{1,0:T(8,128)(2,1)S(1)}, u32[]{:S(2)}, u32[]{:S(2)}) collective-permute-start(bf16[1536,128]{1,0:T(8,128)(2,1)S(1)} %pad_maximum_fusion.1), channel_id=1, source_target_pairs={{0,96},{8,104},{16,112},{24,120},{32,0},{40,8},{48,16},{56,24},{64... | collective-permute-start | bytes 1179656 | tf_op jit(solution)/shard_map/ppermute | solution.py:266
  33.6 6.4 %product_diagonal.1 = (f32[1024,3072]{1,0:T(8,128)S(1)}, f32[1024,128]{1,0:T(8,128)S(1)}) custom-call(bf16[1024,128]{1,0:T(8,128)(2,1)S(1)} %collective-permute-done.8.refs_0_, bf16[1024,128]{1,0:T(8,128)(2,1)S(1)} %collective-permute-done.5.refs_1_, bf16[1024,128]{1,0:T(8,128)(2,1)S(1)} %collective-permute-done.3.refs_2_, ...), custom_call_target="tpu_custom_call", output_to_operand_aliasing={{0}: (6, {})} | custom-call | flops 4026531840 | tf_op jit(solution)/shard_map/product_diagonal/pallas_call | solution.py:245
  40.0 4.6 %product_a.1 = (f32[1024,3072]{1,0:T(8,128)S(1)}, f32[1,3072]{1,0:T(1,128)S(1)}) custom-call(bf16[1536,128]{1,0:T(8,128)(2,1)S(1)} %collective-permute-done.10.refs_0_, bf16[1536,128]{1,0:T(8,128)(2,1)S(1)} %collective-permute-done.11.refs_1_, bf16[3072,2048]{1,0:T(8,128)(2,1)S(1)} %get-tuple-element.24.refs_5_.refs_2_, ...), custom_call_target="tpu_custom_call", output_to_operand_aliasing={{0}: (3, {})} | custom-call | flops 2415919104 | tf_op jit(solution)/shard_map/product_a/pallas_call | solution.py:245
  44.7 4.6 %product_b.1 = (f32[1024,3072]{1,0:T(8,128)S(1)}, f32[1,3072]{1,0:T(1,128)S(1)}) custom-call(bf16[1536,128]{1,0:T(8,128)(2,1)S(1)} %collective-permute-done.4.refs_0_, bf16[1536,128]{1,0:T(8,128)(2,1)S(1)} %collective-permute-done.6.refs_1_, bf16[3072,2048]{1,0:T(8,128)(2,1)S(1)} %get-tuple-element.24.refs_5_.refs_2_, ...), custom_call_target="tpu_custom_call", output_to_operand_aliasing={{0}: (3, {})} | custom-call | flops 2415919104 | tf_op jit(solution)/shard_map/product_b/pallas_call | solution.py:245
  52.3 2.7 %collective-permute-start.15 = (f32[1,3072]{1,0:T(1,128)S(1)}, f32[1,3072]{1,0:T(1,128)S(1)}, u32[]{:S(2)}, u32[]{:S(2)}) collective-permute-start(f32[1,3072]{1,0:T(1,128)S(1)} %compare_select_fusion.refs_1_), channel_id=1, source_target_pairs={{0,4},{1,5},{2,6},{3,7},{4,0},{5,1},{6,2},{7,3},{8,12},{9,13},{10,... | collective-permute-start | bytes 36872 | tf_op jit(solution)/shard_map/ppermute | solution.py:373
  58.7 3.2 %kernel_matrix.1 = (bf16[1024,3072]{1,0:T(8,128)(2,1)S(1)}, f32[1,3072]{1,0:T(1,128)S(1)}, f32[1,1024]{1,0:T(1,128)S(1)}, f32[16,1,1024]{2,1,0:T(1,128)S(1)}) custom-call(f32[1024,3072]{1,0:T(8,128)S(1)} %get-tuple-element.30.refs_0_, f32[1,3072]{1,0:T(1,128)S(1)} %compare_select_fusion.refs_1_, f32[1,3072]{1,0:T(1,128)S(1)} %collective-permute-done.14.refs_2_, ...), custom_call_target="tpu_custom_call" | custom-call | tf_op jit(solution)/shard_map/kernel_matrix/pallas_call | solution.py:438
  61.9 12.1 %all_to_all.15.refs_2_ = f32[16,1,1024]{2,1,0:T(1,128)S(1)} all-to-all(f32[16,1,1024]{2,1,0:T(1,128)S(1)} %get-tuple-element.36), channel_id=1, replica_groups=mesh['train'=16,'val'=8] {'train'}, dimensions={0} | all-to-all | bytes 131072 | tf_op jit(solution)/shard_map/all_to_all | solution.py:382
  76.7 3.8 %collective-permute-start.19 = (f32[1,3072]{1,0:T(1,128)S(1)}, f32[1,3072]{1,0:T(1,128)S(1)}, u32[]{:S(2)}, u32[]{:S(2)}) collective-permute-start(f32[1,3072]{1,0:T(1,128)S(1)} %add.22.refs_2_), channel_id=1, source_target_pairs={{0,4},{1,5},{2,6},{3,7},{4,0},{5,1},{6,2},{7,3},{8,12},{9,13},{10,... | collective-permute-start | bytes 36872 | tf_op jit(solution)/shard_map/ppermute | solution.py:373
  82.3 1.9 %collective-permute-done.20.refs_5_ = f32[1,3072]{1,0:T(1,128)S(1)} collective-permute-done((f32[1,3072]{1,0:T(1,128)S(1)}, f32[1,3072]{1,0:T(1,128)S(1)}, u32[]{:S(2)}, u32[]{:S(2)}) %collective-permute-start.20) | collective-permute-done | bytes 12320 | tf_op jit(solution)/shard_map/ppermute | solution.py:373
  84.2 1.6 %columns.2 = f32[16,1,1024]{2,1,0:T(1,128)S(1)} custom-call(bf16[1024,3072]{1,0:T(8,128)(2,1)S(1)} %get-tuple-element.34.refs_0_, f32[1,1024]{1,0:T(1,128)S(1)} %get-tuple-element.37.refs_1_, f32[1,3072]{1,0:T(1,128)S(1)} %add.22.refs_2_, f32[1,3072]{1,0:T(1,128)S(1)} %collective-permute-done.18.refs_3_, f32[1,3072]{1,0:T(1,128)S(1)} %collective-permute-done.19.refs_4_, ...), custom_call_target="tpu_custom_call" | custom-call | tf_op jit(solution)/shard_map/columns/pallas_call | solution.py:460
  85.8 10.9 %all_to_all.16.refs_2_ = f32[16,1,1024]{2,1,0:T(1,128)S(1)} all-to-all(f32[16,1,1024]{2,1,0:T(1,128)S(1)} %columns.2), channel_id=1, replica_groups=mesh['train'=16,'val'=8] {'train'}, dimensions={0} | all-to-all | bytes 131072 | tf_op jit(solution)/shard_map/all_to_all | solution.py:382
  99.1 2.7 %collective-permute-start.23 = (f32[1,3072]{1,0:T(1,128)S(1)}, f32[1,3072]{1,0:T(1,128)S(1)}, u32[]{:S(2)}, u32[]{:S(2)}) collective-permute-start(f32[1,3072]{1,0:T(1,128)S(1)} %add.23.refs_2_), channel_id=1, source_target_pairs={{0,4},{1,5},{2,6},{3,7},{4,0},{5,1},{6,2},{7,3},{8,12},{9,13},{10,... | collective-permute-start | bytes 36872 | tf_op jit(solution)/shard_map/ppermute | solution.py:373
  105.5 2.2 %columns.3 = f32[16,1,1024]{2,1,0:T(1,128)} custom-call(bf16[1024,3072]{1,0:T(8,128)(2,1)S(1)} %get-tuple-element.34.refs_0_, f32[1,1024]{1,0:T(1,128)S(1)} %get-tuple-element.37.refs_1_, f32[1,3072]{1,0:T(1,128)S(1)} %add.23.refs_2_, f32[1,3072]{1,0:T(1,128)S(1)} %collective-permute-done.22.refs_3_, f32[1,3072]{1,0:T(1,128)S(1)} %collective-permute-done.23.refs_4_, ...), custom_call_target="tpu_custom_call" | custom-call | tf_op jit(solution)/shard_map/columns/pallas_call | solution.py:460
  107.7 3.5 %all-to-all-start.2 = ((f32[16,1,1024]{2,1,0:T(1,128)}), f32[16,1,1024]{2,1,0:T(1,128)S(1)}, u32[]{:S(2)}, u32[]{:S(2)}) async-start(f32[16,1,1024]{2,1,0:T(1,128)} %columns.3), calls=%async_computation.2 | async-start | bytes 131072 | tf_op jit(solution)/shard_map/all_to_all | solution.py:382
  111.2 6.4 %train_potential.1 = f32[1,3072]{1,0:T(1,128)} custom-call(bf16[3072,2048]{1,0:T(8,128)(2,1)} %refs_0_.5, f32[1,3072]{1,0:T(1,128)S(1)} %get-tuple-element.33.refs_1_, f32[1,3072]{1,0:T(1,128)S(1)} %add.23.refs_2_, f32[1,3072]{1,0:T(1,128)S(1)} %collective-permute-done.22.refs_3_, f32[1,3072]{1,0:T(1,128)S(1)} %collective-permute-done.23.refs_4_, ...), custom_call_target="tpu_custom_call" | custom-call | tf_op jit(solution)/shard_map/train_potential/pallas_call | solution.py:480
  (64 shorter events, 22.4 us)
Async XLA Ops:
  0.6 10.8 %collective-permute-start.1 = (bf16[1024,128]{1,0:T(8,128)(2,1)}, bf16[1024,128]{1,0:T(8,128)(2,1)S(1)}, u32[]{:S(2)}, u32[]{:S(2)}) collective-permute-start(bf16[1024,128]{1,0:T(8,128)(2,1)} %refs_0_.4), channel_id=1, source_target_pairs={{0,96},{8,104},{16,112},{24,120},{32,0},{40,8},{48,16},{56,24},{64... | collective-permute-start | bytes 786440 | tf_op jit(solution)/shard_map/ppermute | solution.py:266
  3.8 9.2 %collective-permute-start.2 = (bf16[1024,128]{1,0:T(8,128)(2,1)}, bf16[1024,128]{1,0:T(8,128)(2,1)S(1)}, u32[]{:S(2)}, u32[]{:S(2)}) collective-permute-start(bf16[1024,128]{1,0:T(8,128)(2,1)} %refs_0_.4), channel_id=1, source_target_pairs={{0,32},{8,40},{16,48},{24,56},{32,64},{40,72},{48,80},{56,88},{64,... | collective-permute-start | bytes 786440 | tf_op jit(solution)/shard_map/ppermute | solution.py:266
  3.8 13.4 %collective-permute-start = (bf16[1024,128]{1,0:T(8,128)(2,1)}, bf16[1024,128]{1,0:T(8,128)(2,1)S(1)}, u32[]{:S(2)}, u32[]{:S(2)}) collective-permute-start(bf16[1024,128]{1,0:T(8,128)(2,1)} %refs_0_.4), channel_id=1, source_target_pairs={{0,8},{8,16},{16,24},{24,0},{32,40},{40,48},{48,56},{56,32},{64,72... | collective-permute-start | bytes 786440 | tf_op jit(solution)/shard_map/ppermute | solution.py:266
  5.7 11.5 %collective-permute-start.7 = (bf16[1024,128]{1,0:T(8,128)(2,1)}, bf16[1024,128]{1,0:T(8,128)(2,1)S(1)}, u32[]{:S(2)}, u32[]{:S(2)}) collective-permute-start(bf16[1024,128]{1,0:T(8,128)(2,1)} %refs_0_.4), channel_id=1, source_target_pairs={{0,24},{8,0},{16,8},{24,16},{32,56},{40,32},{48,40},{56,48},{64,88... | collective-permute-start | bytes 786440 | tf_op jit(solution)/shard_map/ppermute | solution.py:266
  13.0 16.9 %collective-permute-start.3 = (bf16[1024,128]{1,0:T(8,128)(2,1)S(1)}, bf16[1024,128]{1,0:T(8,128)(2,1)S(1)}, u32[]{:S(2)}, u32[]{:S(2)}) collective-permute-start(bf16[1024,128]{1,0:T(8,128)(2,1)S(1)} %pad_maximum_fusion.4), channel_id=1, source_target_pairs={{0,8},{8,16},{16,24},{24,0},{32,40},{40,48},{48,56},{56,32},{64,72... | collective-permute-start | bytes 786440 | tf_op jit(solution)/shard_map/ppermute | solution.py:266
  15.0 14.9 %collective-permute-start.5 = (bf16[1024,128]{1,0:T(8,128)(2,1)S(1)}, bf16[1024,128]{1,0:T(8,128)(2,1)S(1)}, u32[]{:S(2)}, u32[]{:S(2)}) collective-permute-start(bf16[1024,128]{1,0:T(8,128)(2,1)S(1)} %pad_maximum_fusion.4), channel_id=1, source_target_pairs={{0,24},{8,0},{16,8},{24,16},{32,56},{40,32},{48,40},{56,48},{64,88... | collective-permute-start | bytes 786440 | tf_op jit(solution)/shard_map/ppermute | solution.py:266
  17.3 9.9 %collective-permute-start.9 = (bf16[1024,128]{1,0:T(8,128)(2,1)S(1)}, bf16[1024,128]{1,0:T(8,128)(2,1)S(1)}, u32[]{:S(2)}, u32[]{:S(2)}) collective-permute-start(bf16[1024,128]{1,0:T(8,128)(2,1)S(1)} %pad_maximum_fusion.5), channel_id=1, source_target_pairs={{0,32},{8,40},{16,48},{24,56},{32,64},{40,72},{48,80},{56,88},{64,... | collective-permute-start | bytes 786440 | tf_op jit(solution)/shard_map/ppermute | solution.py:266
  17.4 9.8 %collective-permute-start.8 = (bf16[1024,128]{1,0:T(8,128)(2,1)S(1)}, bf16[1024,128]{1,0:T(8,128)(2,1)S(1)}, u32[]{:S(2)}, u32[]{:S(2)}) collective-permute-start(bf16[1024,128]{1,0:T(8,128)(2,1)S(1)} %pad_maximum_fusion.5), channel_id=1, source_target_pairs={{0,96},{8,104},{16,112},{24,120},{32,0},{40,8},{48,16},{56,24},{64... | collective-permute-start | bytes 786440 | tf_op jit(solution)/shard_map/ppermute | solution.py:266
  20.6 13.0 %collective-permute-start.12 = (bf16[1024,128]{1,0:T(8,128)(2,1)S(1)}, bf16[1024,128]{1,0:T(8,128)(2,1)S(1)}, u32[]{:S(2)}, u32[]{:S(2)}) collective-permute-start(bf16[1024,128]{1,0:T(8,128)(2,1)S(1)} %collective-permute-done.2.refs_4_), channel_id=1, source_target_pairs={{0,48},{8,56},{16,32},{24,40},{32,80},{40,88},{48,64},{56,72},{64,... | collective-permute-start | bytes 786440 | tf_op jit(solution)/shard_map/ppermute | solution.py:266
  27.2 12.7 %collective-permute-start.10 = (bf16[1536,128]{1,0:T(8,128)(2,1)S(1)}, bf16[1536,128]{1,0:T(8,128)(2,1)S(1)}, u32[]{:S(2)}, u32[]{:S(2)}) collective-permute-start(bf16[1536,128]{1,0:T(8,128)(2,1)S(1)} %pad_maximum_fusion.2), channel_id=1, source_target_pairs={{0,24},{8,0},{16,8},{24,16},{32,56},{40,32},{48,40},{56,48},{64,88... | collective-permute-start | bytes 1179656 | tf_op jit(solution)/shard_map/ppermute | solution.py:266
  29.9 10.1 %collective-permute-start.11 = (bf16[1536,128]{1,0:T(8,128)(2,1)S(1)}, bf16[1536,128]{1,0:T(8,128)(2,1)S(1)}, u32[]{:S(2)}, u32[]{:S(2)}) collective-permute-start(bf16[1536,128]{1,0:T(8,128)(2,1)S(1)} %pad_maximum_fusion.3), channel_id=1, source_target_pairs={{0,32},{8,40},{16,48},{24,56},{32,64},{40,72},{48,80},{56,88},{64,... | collective-permute-start | bytes 1179656 | tf_op jit(solution)/shard_map/ppermute | solution.py:266
  30.0 14.6 %collective-permute-start.6 = (bf16[1536,128]{1,0:T(8,128)(2,1)S(1)}, bf16[1536,128]{1,0:T(8,128)(2,1)S(1)}, u32[]{:S(2)}, u32[]{:S(2)}) collective-permute-start(bf16[1536,128]{1,0:T(8,128)(2,1)S(1)} %pad_maximum_fusion.1), channel_id=1, source_target_pairs={{0,96},{8,104},{16,112},{24,120},{32,0},{40,8},{48,16},{56,24},{64... | collective-permute-start | bytes 1179656 | tf_op jit(solution)/shard_map/ppermute | solution.py:266
  33.3 11.3 %collective-permute-start.4 = (bf16[1536,128]{1,0:T(8,128)(2,1)S(1)}, bf16[1536,128]{1,0:T(8,128)(2,1)S(1)}, u32[]{:S(2)}, u32[]{:S(2)}) collective-permute-start(bf16[1536,128]{1,0:T(8,128)(2,1)S(1)} %pad_maximum_fusion), channel_id=1, source_target_pairs={{0,8},{8,16},{16,24},{24,0},{32,40},{40,48},{48,56},{56,32},{64,72... | collective-permute-start | bytes 1179656 | tf_op jit(solution)/shard_map/ppermute | solution.py:266
  49.4 1.3 %collective-permute-start.13 = (f32[1,3072]{1,0:T(1,128)S(1)}, f32[1,3072]{1,0:T(1,128)S(1)}, u32[]{:S(2)}, u32[]{:S(2)}) collective-permute-start(f32[1,3072]{1,0:T(1,128)S(1)} %compare_select_fusion.1), channel_id=1, source_target_pairs={{0,1},{1,0},{2,3},{3,2},{4,5},{5,4},{6,7},{7,6},{8,9},{9,8},{10,11... | collective-permute-start | bytes 36872 | tf_op jit(solution)/shard_map/ppermute | solution.py:378
  50.7 5.7 %collective-permute-start.14 = (f32[1,3072]{1,0:T(1,128)S(1)}, f32[1,3072]{1,0:T(1,128)S(1)}, u32[]{:S(2)}, u32[]{:S(2)}) collective-permute-start(f32[1,3072]{1,0:T(1,128)S(1)} %compare_select_fusion.refs_1_), channel_id=1, source_target_pairs={{0,2},{1,3},{2,4},{3,5},{4,6},{5,7},{6,0},{7,1},{8,10},{9,11},{10,... | collective-permute-start | bytes 36872 | tf_op jit(solution)/shard_map/ppermute | solution.py:373
  52.3 5.2 %collective-permute-start.15 = (f32[1,3072]{1,0:T(1,128)S(1)}, f32[1,3072]{1,0:T(1,128)S(1)}, u32[]{:S(2)}, u32[]{:S(2)}) collective-permute-start(f32[1,3072]{1,0:T(1,128)S(1)} %compare_select_fusion.refs_1_), channel_id=1, source_target_pairs={{0,4},{1,5},{2,6},{3,7},{4,0},{5,1},{6,2},{7,3},{8,12},{9,13},{10,... | collective-permute-start | bytes 36872 | tf_op jit(solution)/shard_map/ppermute | solution.py:373
  55.0 3.7 %collective-permute-start.16 = (f32[1,3072]{1,0:T(1,128)S(1)}, f32[1,3072]{1,0:T(1,128)S(1)}, u32[]{:S(2)}, u32[]{:S(2)}) collective-permute-start(f32[1,3072]{1,0:T(1,128)S(1)} %compare_select_fusion.refs_1_), channel_id=1, source_target_pairs={{0,6},{1,7},{2,0},{3,1},{4,2},{5,3},{6,4},{7,5},{8,14},{9,15},{10,... | collective-permute-start | bytes 36872 | tf_op jit(solution)/shard_map/ppermute | solution.py:373
  76.3 5.0 %collective-permute-start.18 = (f32[1,3072]{1,0:T(1,128)S(1)}, f32[1,3072]{1,0:T(1,128)S(1)}, u32[]{:S(2)}, u32[]{:S(2)}) collective-permute-start(f32[1,3072]{1,0:T(1,128)S(1)} %add.22.refs_2_), channel_id=1, source_target_pairs={{0,2},{1,3},{2,4},{3,5},{4,6},{5,7},{6,0},{7,1},{8,10},{9,11},{10,... | collective-permute-start | bytes 36872 | tf_op jit(solution)/shard_map/ppermute | solution.py:373
  76.7 5.6 %collective-permute-start.19 = (f32[1,3072]{1,0:T(1,128)S(1)}, f32[1,3072]{1,0:T(1,128)S(1)}, u32[]{:S(2)}, u32[]{:S(2)}) collective-permute-start(f32[1,3072]{1,0:T(1,128)S(1)} %add.22.refs_2_), channel_id=1, source_target_pairs={{0,4},{1,5},{2,6},{3,7},{4,0},{5,1},{6,2},{7,3},{8,12},{9,13},{10,... | collective-permute-start | bytes 36872 | tf_op jit(solution)/shard_map/ppermute | solution.py:373
  80.5 3.7 %collective-permute-start.20 = (f32[1,3072]{1,0:T(1,128)S(1)}, f32[1,3072]{1,0:T(1,128)S(1)}, u32[]{:S(2)}, u32[]{:S(2)}) collective-permute-start(f32[1,3072]{1,0:T(1,128)S(1)} %add.22.refs_2_), channel_id=1, source_target_pairs={{0,6},{1,7},{2,0},{3,1},{4,2},{5,3},{6,4},{7,5},{8,14},{9,15},{10,... | collective-permute-start | bytes 36872 | tf_op jit(solution)/shard_map/ppermute | solution.py:373
  99.0 5.0 %collective-permute-start.22 = (f32[1,3072]{1,0:T(1,128)S(1)}, f32[1,3072]{1,0:T(1,128)S(1)}, u32[]{:S(2)}, u32[]{:S(2)}) collective-permute-start(f32[1,3072]{1,0:T(1,128)S(1)} %add.23.refs_2_), channel_id=1, source_target_pairs={{0,2},{1,3},{2,4},{3,5},{4,6},{5,7},{6,0},{7,1},{8,10},{9,11},{10,... | collective-permute-start | bytes 36872 | tf_op jit(solution)/shard_map/ppermute | solution.py:373
  99.1 5.3 %collective-permute-start.23 = (f32[1,3072]{1,0:T(1,128)S(1)}, f32[1,3072]{1,0:T(1,128)S(1)}, u32[]{:S(2)}, u32[]{:S(2)}) collective-permute-start(f32[1,3072]{1,0:T(1,128)S(1)} %add.23.refs_2_), channel_id=1, source_target_pairs={{0,4},{1,5},{2,6},{3,7},{4,0},{5,1},{6,2},{7,3},{8,12},{9,13},{10,... | collective-permute-start | bytes 36872 | tf_op jit(solution)/shard_map/ppermute | solution.py:373
  101.8 3.7 %collective-permute-start.24 = (f32[1,3072]{1,0:T(1,128)S(1)}, f32[1,3072]{1,0:T(1,128)S(1)}, u32[]{:S(2)}, u32[]{:S(2)}) collective-permute-start(f32[1,3072]{1,0:T(1,128)S(1)} %add.23.refs_2_), channel_id=1, source_target_pairs={{0,6},{1,7},{2,0},{3,1},{4,2},{5,3},{6,4},{7,5},{8,14},{9,15},{10,... | collective-permute-start | bytes 36872 | tf_op jit(solution)/shard_map/ppermute | solution.py:373
  107.7 11.1 %all-to-all-start.2 = ((f32[16,1,1024]{2,1,0:T(1,128)}), f32[16,1,1024]{2,1,0:T(1,128)S(1)}, u32[]{:S(2)}, u32[]{:S(2)}) async-start(f32[16,1,1024]{2,1,0:T(1,128)} %columns.3), calls=%async_computation.2 | async-start | bytes 131072 | tf_op jit(solution)/shard_map/all_to_all | solution.py:382
  (3 other events, 22.6 us)

commit v4 on v3

--- a/solution.py
+++ b/solution.py
@@ -307,7 +307,7 @@
     row_pot[...] = pot
     block = 128
 
-    @pl.loop(0, cols // block, unroll=4)
+    @pl.loop(0, cols // block, unroll=8)
     def _(k):
         part = pl.ds(pl.multiple_of(k * block, block), block)
         peak = None

time: 120 us -> 120 us (level)
  no operation moved by 1% of the time
where the time goes in v4:
time: 120 us; the launch traced here: 119 us
  Pallas kernels  40 us (33%)
  starting transfers between devices  38.8 us (32%)
  blocking collectives  23 us (19%)
  waiting for transfers between devices  15.5 us (13%)
    all_to_all x2, blocking collectives, spread(): return lax.all_to_all(x, 'train', 0, 0)  23 us
    pallas_call x4, Pallas kernels, product_part(): pl.pallas_call(lambda *refs: part_kernel(plan, len(vals), row, tile, alph...  21 us
    ppermute x13, starting transfers between devices, from_step(): return lax.ppermute(x, 'train', pairs)  21 us
    ppermute x9, starting transfers between devices, other_chips(): lax.ppermute(x, 'val', [(i, (i + 2 * k) % n) for i in range(n)])  14.1 us
    ppermute x9, waiting for transfers between devices, other_chips(): lax.ppermute(x, 'val', [(i, (i + 2 * k) % n) for i in range(n)])  8.17 us
    pallas_call x1, Pallas kernels, shards(): pl.pallas_call(lambda *refs: train_kernel(256, math.log2(total_cols), *re...  6.37 us
    pallas_call x2, Pallas kernels, shards(): pl.pallas_call(lambda *refs: cols_kernel(total_cols, *refs), out_shape=sh...  3.82 us
    pallas_call x1, Pallas kernels, shards(): pl.pallas_call(lambda *refs: prepare_kernel(features, 512, *refs), out_sh...  3.57 us
  transfers between devices with their start and end apart: 26, of which 14 were waited for; matrix products, arithmetic and copies ran while one was open for 0% of the time, Pallas kernels for 22%

profile of v4, /device:TPU:0, one launch (start us, length us, event | category | flops | bytes accessed | tf_op | source)
XLA Modules:
  0.0 119.4 jit_solution(2619993679339806916)
XLA Ops:
  0.6 3.2 %collective-permute-start.1 = (bf16[1024,128]{1,0:T(8,128)(2,1)}, bf16[1024,128]{1,0:T(8,128)(2,1)S(1)}, u32[]{:S(2)}, u32[]{:S(2)}) collective-permute-start(bf16[1024,128]{1,0:T(8,128)(2,1)} %refs_0_.4), channel_id=1, source_target_pairs={{0,96},{8,104},{16,112},{24,120},{32,0},{40,8},{48,16},{56,24},{64... | collective-permute-start | bytes 786440 | tf_op jit(solution)/shard_map/ppermute | solution.py:266
  3.8 1.9 %collective-permute-start = (bf16[1024,128]{1,0:T(8,128)(2,1)}, bf16[1024,128]{1,0:T(8,128)(2,1)S(1)}, u32[]{:S(2)}, u32[]{:S(2)}) collective-permute-start(bf16[1024,128]{1,0:T(8,128)(2,1)} %refs_0_.4), channel_id=1, source_target_pairs={{0,8},{8,16},{16,24},{24,0},{32,40},{40,48},{48,56},{56,32},{64,72... | collective-permute-start | bytes 786440 | tf_op jit(solution)/shard_map/ppermute | solution.py:266
  5.7 2.1 %collective-permute-start.7 = (bf16[1024,128]{1,0:T(8,128)(2,1)}, bf16[1024,128]{1,0:T(8,128)(2,1)S(1)}, u32[]{:S(2)}, u32[]{:S(2)}) collective-permute-start(bf16[1024,128]{1,0:T(8,128)(2,1)} %refs_0_.4), channel_id=1, source_target_pairs={{0,24},{8,0},{16,8},{24,16},{32,56},{40,32},{48,40},{56,48},{64,88... | collective-permute-start | bytes 786440 | tf_op jit(solution)/shard_map/ppermute | solution.py:266
  7.9 3.6 %prepare.1 = (bf16[3072,2048]{1,0:T(8,128)(2,1)S(1)}, bf16[3072,128]{1,0:T(8,128)(2,1)S(1)}, bf16[1024,128]{1,0:T(8,128)(2,1)S(1)}) custom-call(f32[10,10]{1,0:T(8,128)} %refs_0_.3, s32[1,3072]{1,0:T(1,128)} %bitcast.6, s32[1,1024]{1,0:T(1,128)} %bitcast.8, bf16[3072,2048]{1,0:T(8,128)(2,1)} %refs_0_.5), custom_call_target="tpu_custom_call" | custom-call | tf_op jit(solution)/shard_map/prepare/pallas_call | solution.py:395
  13.0 2.0 %collective-permute-start.3 = (bf16[1024,128]{1,0:T(8,128)(2,1)S(1)}, bf16[1024,128]{1,0:T(8,128)(2,1)S(1)}, u32[]{:S(2)}, u32[]{:S(2)}) collective-permute-start(bf16[1024,128]{1,0:T(8,128)(2,1)S(1)} %pad_maximum_fusion.4), channel_id=1, source_target_pairs={{0,8},{8,16},{16,24},{24,0},{32,40},{40,48},{48,56},{56,32},{64,72... | collective-permute-start | bytes 786440 | tf_op jit(solution)/shard_map/ppermute | solution.py:266
  15.0 2.2 %collective-permute-start.5 = (bf16[1024,128]{1,0:T(8,128)(2,1)S(1)}, bf16[1024,128]{1,0:T(8,128)(2,1)S(1)}, u32[]{:S(2)}, u32[]{:S(2)}) collective-permute-start(bf16[1024,128]{1,0:T(8,128)(2,1)S(1)} %pad_maximum_fusion.4), channel_id=1, source_target_pairs={{0,24},{8,0},{16,8},{24,16},{32,56},{40,32},{48,40},{56,48},{64,88... | collective-permute-start | bytes 786440 | tf_op jit(solution)/shard_map/ppermute | solution.py:266
  17.4 3.2 %collective-permute-start.8 = (bf16[1024,128]{1,0:T(8,128)(2,1)S(1)}, bf16[1024,128]{1,0:T(8,128)(2,1)S(1)}, u32[]{:S(2)}, u32[]{:S(2)}) collective-permute-start(bf16[1024,128]{1,0:T(8,128)(2,1)S(1)} %pad_maximum_fusion.5), channel_id=1, source_target_pairs={{0,96},{8,104},{16,112},{24,120},{32,0},{40,8},{48,16},{56,24},{64... | collective-permute-start | bytes 786440 | tf_op jit(solution)/shard_map/ppermute | solution.py:266
  20.7 5.4 %product_near.1 = (f32[1024,3072]{1,0:T(8,128)S(1)}, f32[1024,128]{1,0:T(8,128)S(1)}, bf16[3072,2048]{1,0:T(8,128)(2,1)S(1)}) custom-call(bf16[1024,128]{1,0:T(8,128)(2,1)S(1)} %copy-done, bf16[1024,128]{1,0:T(8,128)(2,1)S(1)} %collective-permute-done.7.refs_1_, bf16[1024,128]{1,0:T(8,128)(2,1)S(1)} %collective-permute-done.refs_2_, ...), custom_call_target="tpu_custom_call", output_to_operand_aliasing={{2}: (5, {})} | custom-call | flops 4026531840 | tf_op jit(solution)/shard_map/product_near/pallas_call | solution.py:245
  27.2 2.6 %collective-permute-start.10 = (bf16[1536,128]{1,0:T(8,128)(2,1)S(1)}, bf16[1536,128]{1,0:T(8,128)(2,1)S(1)}, u32[]{:S(2)}, u32[]{:S(2)}) collective-permute-start(bf16[1536,128]{1,0:T(8,128)(2,1)S(1)} %pad_maximum_fusion.2), channel_id=1, source_target_pairs={{0,24},{8,0},{16,8},{24,16},{32,56},{40,32},{48,40},{56,48},{64,88... | collective-permute-start | bytes 1179656 | tf_op jit(solution)/shard_map/ppermute | solution.py:266
  30.0 3.3 %collective-permute-start.6 = (bf16[1536,128]{1,0:T(8,128)(2,1)S(1)}, bf16[1536,128]{1,0:T(8,128)(2,1)S(1)}, u32[]{:S(2)}, u32[]{:S(2)}) collective-permute-start(bf16[1536,128]{1,0:T(8,128)(2,1)S(1)} %pad_maximum_fusion.1), channel_id=1, source_target_pairs={{0,96},{8,104},{16,112},{24,120},{32,0},{40,8},{48,16},{56,24},{64... | collective-permute-start | bytes 1179656 | tf_op jit(solution)/shard_map/ppermute | solution.py:266
  33.6 6.4 %product_diagonal.1 = (f32[1024,3072]{1,0:T(8,128)S(1)}, f32[1024,128]{1,0:T(8,128)S(1)}) custom-call(bf16[1024,128]{1,0:T(8,128)(2,1)S(1)} %collective-permute-done.8.refs_0_, bf16[1024,128]{1,0:T(8,128)(2,1)S(1)} %collective-permute-done.5.refs_1_, bf16[1024,128]{1,0:T(8,128)(2,1)S(1)} %collective-permute-done.3.refs_2_, ...), custom_call_target="tpu_custom_call", output_to_operand_aliasing={{0}: (6, {})} | custom-call | flops 4026531840 | tf_op jit(solution)/shard_map/product_diagonal/pallas_call | solution.py:245
  40.0 4.6 %product_a.1 = (f32[1024,3072]{1,0:T(8,128)S(1)}, f32[1,3072]{1,0:T(1,128)S(1)}) custom-call(bf16[1536,128]{1,0:T(8,128)(2,1)S(1)} %collective-permute-done.10.refs_0_, bf16[1536,128]{1,0:T(8,128)(2,1)S(1)} %collective-permute-done.11.refs_1_, bf16[3072,2048]{1,0:T(8,128)(2,1)S(1)} %get-tuple-element.24.refs_5_.refs_2_, ...), custom_call_target="tpu_custom_call", output_to_operand_aliasing={{0}: (3, {})} | custom-call | flops 2415919104 | tf_op jit(solution)/shard_map/product_a/pallas_call | solution.py:245
  44.7 4.6 %product_b.1 = (f32[1024,3072]{1,0:T(8,128)S(1)}, f32[1,3072]{1,0:T(1,128)S(1)}) custom-call(bf16[1536,128]{1,0:T(8,128)(2,1)S(1)} %collective-permute-done.4.refs_0_, bf16[1536,128]{1,0:T(8,128)(2,1)S(1)} %collective-permute-done.6.refs_1_, bf16[3072,2048]{1,0:T(8,128)(2,1)S(1)} %get-tuple-element.24.refs_5_.refs_2_, ...), custom_call_target="tpu_custom_call", output_to_operand_aliasing={{0}: (3, {})} | custom-call | flops 2415919104 | tf_op jit(solution)/shard_map/product_b/pallas_call | solution.py:245
  52.3 2.7 %collective-permute-start.15 = (f32[1,3072]{1,0:T(1,128)S(1)}, f32[1,3072]{1,0:T(1,128)S(1)}, u32[]{:S(2)}, u32[]{:S(2)}) collective-permute-start(f32[1,3072]{1,0:T(1,128)S(1)} %compare_select_fusion.refs_1_), channel_id=1, source_target_pairs={{0,4},{1,5},{2,6},{3,7},{4,0},{5,1},{6,2},{7,3},{8,12},{9,13},{10,... | collective-permute-start | bytes 36872 | tf_op jit(solution)/shard_map/ppermute | solution.py:373
  58.7 3.2 %kernel_matrix.1 = (bf16[1024,3072]{1,0:T(8,128)(2,1)S(1)}, f32[1,3072]{1,0:T(1,128)S(1)}, f32[1,1024]{1,0:T(1,128)S(1)}, f32[16,1,1024]{2,1,0:T(1,128)S(1)}) custom-call(f32[1024,3072]{1,0:T(8,128)S(1)} %get-tuple-element.30.refs_0_, f32[1,3072]{1,0:T(1,128)S(1)} %compare_select_fusion.refs_1_, f32[1,3072]{1,0:T(1,128)S(1)} %collective-permute-done.14.refs_2_, ...), custom_call_target="tpu_custom_call" | custom-call | tf_op jit(solution)/shard_map/kernel_matrix/pallas_call | solution.py:438
  61.9 12.1 %all_to_all.15.refs_2_ = f32[16,1,1024]{2,1,0:T(1,128)S(1)} all-to-all(f32[16,1,1024]{2,1,0:T(1,128)S(1)} %get-tuple-element.36), channel_id=1, replica_groups=mesh['train'=16,'val'=8] {'train'}, dimensions={0} | all-to-all | bytes 131072 | tf_op jit(solution)/shard_map/all_to_all | solution.py:382
  76.6 3.8 %collective-permute-start.19 = (f32[1,3072]{1,0:T(1,128)S(1)}, f32[1,3072]{1,0:T(1,128)S(1)}, u32[]{:S(2)}, u32[]{:S(2)}) collective-permute-start(f32[1,3072]{1,0:T(1,128)S(1)} %add.22.refs_2_), channel_id=1, source_target_pairs={{0,4},{1,5},{2,6},{3,7},{4,0},{5,1},{6,2},{7,3},{8,12},{9,13},{10,... | collective-permute-start | bytes 36872 | tf_op jit(solution)/shard_map/ppermute | solution.py:373
  82.3 1.9 %collective-permute-done.20.refs_5_ = f32[1,3072]{1,0:T(1,128)S(1)} collective-permute-done((f32[1,3072]{1,0:T(1,128)S(1)}, f32[1,3072]{1,0:T(1,128)S(1)}, u32[]{:S(2)}, u32[]{:S(2)}) %collective-permute-start.20) | collective-permute-done | bytes 12320 | tf_op jit(solution)/shard_map/ppermute | solution.py:373
  84.1 1.6 %columns.2 = f32[16,1,1024]{2,1,0:T(1,128)S(1)} custom-call(bf16[1024,3072]{1,0:T(8,128)(2,1)S(1)} %get-tuple-element.34.refs_0_, f32[1,1024]{1,0:T(1,128)S(1)} %get-tuple-element.37.refs_1_, f32[1,3072]{1,0:T(1,128)S(1)} %add.22.refs_2_, f32[1,3072]{1,0:T(1,128)S(1)} %collective-permute-done.18.refs_3_, f32[1,3072]{1,0:T(1,128)S(1)} %collective-permute-done.19.refs_4_, ...), custom_call_target="tpu_custom_call" | custom-call | tf_op jit(solution)/shard_map/columns/pallas_call | solution.py:460
  85.7 10.9 %all_to_all.16.refs_2_ = f32[16,1,1024]{2,1,0:T(1,128)S(1)} all-to-all(f32[16,1,1024]{2,1,0:T(1,128)S(1)} %columns.2), channel_id=1, replica_groups=mesh['train'=16,'val'=8] {'train'}, dimensions={0} | all-to-all | bytes 131072 | tf_op jit(solution)/shard_map/all_to_all | solution.py:382
  99.0 2.7 %collective-permute-start.23 = (f32[1,3072]{1,0:T(1,128)S(1)}, f32[1,3072]{1,0:T(1,128)S(1)}, u32[]{:S(2)}, u32[]{:S(2)}) collective-permute-start(f32[1,3072]{1,0:T(1,128)S(1)} %add.23.refs_2_), channel_id=1, source_target_pairs={{0,4},{1,5},{2,6},{3,7},{4,0},{5,1},{6,2},{7,3},{8,12},{9,13},{10,... | collective-permute-start | bytes 36872 | tf_op jit(solution)/shard_map/ppermute | solution.py:373
  105.4 2.2 %columns.3 = f32[16,1,1024]{2,1,0:T(1,128)} custom-call(bf16[1024,3072]{1,0:T(8,128)(2,1)S(1)} %get-tuple-element.34.refs_0_, f32[1,1024]{1,0:T(1,128)S(1)} %get-tuple-element.37.refs_1_, f32[1,3072]{1,0:T(1,128)S(1)} %add.23.refs_2_, f32[1,3072]{1,0:T(1,128)S(1)} %collective-permute-done.22.refs_3_, f32[1,3072]{1,0:T(1,128)S(1)} %collective-permute-done.23.refs_4_, ...), custom_call_target="tpu_custom_call" | custom-call | tf_op jit(solution)/shard_map/columns/pallas_call | solution.py:460
  107.6 3.5 %all-to-all-start.2 = ((f32[16,1,1024]{2,1,0:T(1,128)}), f32[16,1,1024]{2,1,0:T(1,128)S(1)}, u32[]{:S(2)}, u32[]{:S(2)}) async-start(f32[16,1,1024]{2,1,0:T(1,128)} %columns.3), calls=%async_computation.2 | async-start | bytes 131072 | tf_op jit(solution)/shard_map/all_to_all | solution.py:382
  111.1 6.4 %train_potential.1 = f32[1,3072]{1,0:T(1,128)} custom-call(bf16[3072,2048]{1,0:T(8,128)(2,1)} %refs_0_.5, f32[1,3072]{1,0:T(1,128)S(1)} %get-tuple-element.33.refs_1_, f32[1,3072]{1,0:T(1,128)S(1)} %add.23.refs_2_, f32[1,3072]{1,0:T(1,128)S(1)} %collective-permute-done.22.refs_3_, f32[1,3072]{1,0:T(1,128)S(1)} %collective-permute-done.23.refs_4_, ...), custom_call_target="tpu_custom_call" | custom-call | tf_op jit(solution)/shard_map/train_potential/pallas_call | solution.py:480
  (64 shorter events, 22.4 us)
Async XLA Ops:
  0.6 10.8 %collective-permute-start.1 = (bf16[1024,128]{1,0:T(8,128)(2,1)}, bf16[1024,128]{1,0:T(8,128)(2,1)S(1)}, u32[]{:S(2)}, u32[]{:S(2)}) collective-permute-start(bf16[1024,128]{1,0:T(8,128)(2,1)} %refs_0_.4), channel_id=1, source_target_pairs={{0,96},{8,104},{16,112},{24,120},{32,0},{40,8},{48,16},{56,24},{64... | collective-permute-start | bytes 786440 | tf_op jit(solution)/shard_map/ppermute | solution.py:266
  3.8 9.2 %collective-permute-start.2 = (bf16[1024,128]{1,0:T(8,128)(2,1)}, bf16[1024,128]{1,0:T(8,128)(2,1)S(1)}, u32[]{:S(2)}, u32[]{:S(2)}) collective-permute-start(bf16[1024,128]{1,0:T(8,128)(2,1)} %refs_0_.4), channel_id=1, source_target_pairs={{0,32},{8,40},{16,48},{24,56},{32,64},{40,72},{48,80},{56,88},{64,... | collective-permute-start | bytes 786440 | tf_op jit(solution)/shard_map/ppermute | solution.py:266
  3.8 13.4 %collective-permute-start = (bf16[1024,128]{1,0:T(8,128)(2,1)}, bf16[1024,128]{1,0:T(8,128)(2,1)S(1)}, u32[]{:S(2)}, u32[]{:S(2)}) collective-permute-start(bf16[1024,128]{1,0:T(8,128)(2,1)} %refs_0_.4), channel_id=1, source_target_pairs={{0,8},{8,16},{16,24},{24,0},{32,40},{40,48},{48,56},{56,32},{64,72... | collective-permute-start | bytes 786440 | tf_op jit(solution)/shard_map/ppermute | solution.py:266
  5.7 11.5 %collective-permute-start.7 = (bf16[1024,128]{1,0:T(8,128)(2,1)}, bf16[1024,128]{1,0:T(8,128)(2,1)S(1)}, u32[]{:S(2)}, u32[]{:S(2)}) collective-permute-start(bf16[1024,128]{1,0:T(8,128)(2,1)} %refs_0_.4), channel_id=1, source_target_pairs={{0,24},{8,0},{16,8},{24,16},{32,56},{40,32},{48,40},{56,48},{64,88... | collective-permute-start | bytes 786440 | tf_op jit(solution)/shard_map/ppermute | solution.py:266
  13.0 16.9 %collective-permute-start.3 = (bf16[1024,128]{1,0:T(8,128)(2,1)S(1)}, bf16[1024,128]{1,0:T(8,128)(2,1)S(1)}, u32[]{:S(2)}, u32[]{:S(2)}) collective-permute-start(bf16[1024,128]{1,0:T(8,128)(2,1)S(1)} %pad_maximum_fusion.4), channel_id=1, source_target_pairs={{0,8},{8,16},{16,24},{24,0},{32,40},{40,48},{48,56},{56,32},{64,72... | collective-permute-start | bytes 786440 | tf_op jit(solution)/shard_map/ppermute | solution.py:266
  15.0 14.9 %collective-permute-start.5 = (bf16[1024,128]{1,0:T(8,128)(2,1)S(1)}, bf16[1024,128]{1,0:T(8,128)(2,1)S(1)}, u32[]{:S(2)}, u32[]{:S(2)}) collective-permute-start(bf16[1024,128]{1,0:T(8,128)(2,1)S(1)} %pad_maximum_fusion.4), channel_id=1, source_target_pairs={{0,24},{8,0},{16,8},{24,16},{32,56},{40,32},{48,40},{56,48},{64,88... | collective-permute-start | bytes 786440 | tf_op jit(solution)/shard_map/ppermute | solution.py:266
  17.3 9.9 %collective-permute-start.9 = (bf16[1024,128]{1,0:T(8,128)(2,1)S(1)}, bf16[1024,128]{1,0:T(8,128)(2,1)S(1)}, u32[]{:S(2)}, u32[]{:S(2)}) collective-permute-start(bf16[1024,128]{1,0:T(8,128)(2,1)S(1)} %pad_maximum_fusion.5), channel_id=1, source_target_pairs={{0,32},{8,40},{16,48},{24,56},{32,64},{40,72},{48,80},{56,88},{64,... | collective-permute-start | bytes 786440 | tf_op jit(solution)/shard_map/ppermute | solution.py:266
  17.4 9.8 %collective-permute-start.8 = (bf16[1024,128]{1,0:T(8,128)(2,1)S(1)}, bf16[1024,128]{1,0:T(8,128)(2,1)S(1)}, u32[]{:S(2)}, u32[]{:S(2)}) collective-permute-start(bf16[1024,128]{1,0:T(8,128)(2,1)S(1)} %pad_maximum_fusion.5), channel_id=1, source_target_pairs={{0,96},{8,104},{16,112},{24,120},{32,0},{40,8},{48,16},{56,24},{64... | collective-permute-start | bytes 786440 | tf_op jit(solution)/shard_map/ppermute | solution.py:266
  20.6 13.0 %collective-permute-start.12 = (bf16[1024,128]{1,0:T(8,128)(2,1)S(1)}, bf16[1024,128]{1,0:T(8,128)(2,1)S(1)}, u32[]{:S(2)}, u32[]{:S(2)}) collective-permute-start(bf16[1024,128]{1,0:T(8,128)(2,1)S(1)} %collective-permute-done.2.refs_4_), channel_id=1, source_target_pairs={{0,48},{8,56},{16,32},{24,40},{32,80},{40,88},{48,64},{56,72},{64,... | collective-permute-start | bytes 786440 | tf_op jit(solution)/shard_map/ppermute | solution.py:266
  27.2 12.7 %collective-permute-start.10 = (bf16[1536,128]{1,0:T(8,128)(2,1)S(1)}, bf16[1536,128]{1,0:T(8,128)(2,1)S(1)}, u32[]{:S(2)}, u32[]{:S(2)}) collective-permute-start(bf16[1536,128]{1,0:T(8,128)(2,1)S(1)} %pad_maximum_fusion.2), channel_id=1, source_target_pairs={{0,24},{8,0},{16,8},{24,16},{32,56},{40,32},{48,40},{56,48},{64,88... | collective-permute-start | bytes 1179656 | tf_op jit(solution)/shard_map/ppermute | solution.py:266
  29.9 10.1 %collective-permute-start.11 = (bf16[1536,128]{1,0:T(8,128)(2,1)S(1)}, bf16[1536,128]{1,0:T(8,128)(2,1)S(1)}, u32[]{:S(2)}, u32[]{:S(2)}) collective-permute-start(bf16[1536,128]{1,0:T(8,128)(2,1)S(1)} %pad_maximum_fusion.3), channel_id=1, source_target_pairs={{0,32},{8,40},{16,48},{24,56},{32,64},{40,72},{48,80},{56,88},{64,... | collective-permute-start | bytes 1179656 | tf_op jit(solution)/shard_map/ppermute | solution.py:266
  30.0 14.6 %collective-permute-start.6 = (bf16[1536,128]{1,0:T(8,128)(2,1)S(1)}, bf16[1536,128]{1,0:T(8,128)(2,1)S(1)}, u32[]{:S(2)}, u32[]{:S(2)}) collective-permute-start(bf16[1536,128]{1,0:T(8,128)(2,1)S(1)} %pad_maximum_fusion.1), channel_id=1, source_target_pairs={{0,96},{8,104},{16,112},{24,120},{32,0},{40,8},{48,16},{56,24},{64... | collective-permute-start | bytes 1179656 | tf_op jit(solution)/shard_map/ppermute | solution.py:266
  33.3 11.3 %collective-permute-start.4 = (bf16[1536,128]{1,0:T(8,128)(2,1)S(1)}, bf16[1536,128]{1,0:T(8,128)(2,1)S(1)}, u32[]{:S(2)}, u32[]{:S(2)}) collective-permute-start(bf16[1536,128]{1,0:T(8,128)(2,1)S(1)} %pad_maximum_fusion), channel_id=1, source_target_pairs={{0,8},{8,16},{16,24},{24,0},{32,40},{40,48},{48,56},{56,32},{64,72... | collective-permute-start | bytes 1179656 | tf_op jit(solution)/shard_map/ppermute | solution.py:266
  50.7 5.7 %collective-permute-start.14 = (f32[1,3072]{1,0:T(1,128)S(1)}, f32[1,3072]{1,0:T(1,128)S(1)}, u32[]{:S(2)}, u32[]{:S(2)}) collective-permute-start(f32[1,3072]{1,0:T(1,128)S(1)} %compare_select_fusion.refs_1_), channel_id=1, source_target_pairs={{0,2},{1,3},{2,4},{3,5},{4,6},{5,7},{6,0},{7,1},{8,10},{9,11},{10,... | collective-permute-start | bytes 36872 | tf_op jit(solution)/shard_map/ppermute | solution.py:373
  52.3 5.2 %collective-permute-start.15 = (f32[1,3072]{1,0:T(1,128)S(1)}, f32[1,3072]{1,0:T(1,128)S(1)}, u32[]{:S(2)}, u32[]{:S(2)}) collective-permute-start(f32[1,3072]{1,0:T(1,128)S(1)} %compare_select_fusion.refs_1_), channel_id=1, source_target_pairs={{0,4},{1,5},{2,6},{3,7},{4,0},{5,1},{6,2},{7,3},{8,12},{9,13},{10,... | collective-permute-start | bytes 36872 | tf_op jit(solution)/shard_map/ppermute | solution.py:373
  55.0 3.7 %collective-permute-start.16 = (f32[1,3072]{1,0:T(1,128)S(1)}, f32[1,3072]{1,0:T(1,128)S(1)}, u32[]{:S(2)}, u32[]{:S(2)}) collective-permute-start(f32[1,3072]{1,0:T(1,128)S(1)} %compare_select_fusion.refs_1_), channel_id=1, source_target_pairs={{0,6},{1,7},{2,0},{3,1},{4,2},{5,3},{6,4},{7,5},{8,14},{9,15},{10,... | collective-permute-start | bytes 36872 | tf_op jit(solution)/shard_map/ppermute | solution.py:373
  75.0 1.3 %collective-permute-start.17 = (f32[1,3072]{1,0:T(1,128)S(1)}, f32[1,3072]{1,0:T(1,128)S(1)}, u32[]{:S(2)}, u32[]{:S(2)}) collective-permute-start(f32[1,3072]{1,0:T(1,128)S(1)} %get-tuple-element.38), channel_id=1, source_target_pairs={{0,1},{1,0},{2,3},{3,2},{4,5},{5,4},{6,7},{7,6},{8,9},{9,8},{10,11... | collective-permute-start | bytes 36872 | tf_op jit(solution)/shard_map/ppermute | solution.py:378
  76.3 5.0 %collective-permute-start.18 = (f32[1,3072]{1,0:T(1,128)S(1)}, f32[1,3072]{1,0:T(1,128)S(1)}, u32[]{:S(2)}, u32[]{:S(2)}) collective-permute-start(f32[1,3072]{1,0:T(1,128)S(1)} %add.22.refs_2_), channel_id=1, source_target_pairs={{0,2},{1,3},{2,4},{3,5},{4,6},{5,7},{6,0},{7,1},{8,10},{9,11},{10,... | collective-permute-start | bytes 36872 | tf_op jit(solution)/shard_map/ppermute | solution.py:373
  76.6 5.6 %collective-permute-start.19 = (f32[1,3072]{1,0:T(1,128)S(1)}, f32[1,3072]{1,0:T(1,128)S(1)}, u32[]{:S(2)}, u32[]{:S(2)}) collective-permute-start(f32[1,3072]{1,0:T(1,128)S(1)} %add.22.refs_2_), channel_id=1, source_target_pairs={{0,4},{1,5},{2,6},{3,7},{4,0},{5,1},{6,2},{7,3},{8,12},{9,13},{10,... | collective-permute-start | bytes 36872 | tf_op jit(solution)/shard_map/ppermute | solution.py:373
  80.5 3.7 %collective-permute-start.20 = (f32[1,3072]{1,0:T(1,128)S(1)}, f32[1,3072]{1,0:T(1,128)S(1)}, u32[]{:S(2)}, u32[]{:S(2)}) collective-permute-start(f32[1,3072]{1,0:T(1,128)S(1)} %add.22.refs_2_), channel_id=1, source_target_pairs={{0,6},{1,7},{2,0},{3,1},{4,2},{5,3},{6,4},{7,5},{8,14},{9,15},{10,... | collective-permute-start | bytes 36872 | tf_op jit(solution)/shard_map/ppermute | solution.py:373
  98.9 5.0 %collective-permute-start.22 = (f32[1,3072]{1,0:T(1,128)S(1)}, f32[1,3072]{1,0:T(1,128)S(1)}, u32[]{:S(2)}, u32[]{:S(2)}) collective-permute-start(f32[1,3072]{1,0:T(1,128)S(1)} %add.23.refs_2_), channel_id=1, source_target_pairs={{0,2},{1,3},{2,4},{3,5},{4,6},{5,7},{6,0},{7,1},{8,10},{9,11},{10,... | collective-permute-start | bytes 36872 | tf_op jit(solution)/shard_map/ppermute | solution.py:373
  99.0 5.3 %collective-permute-start.23 = (f32[1,3072]{1,0:T(1,128)S(1)}, f32[1,3072]{1,0:T(1,128)S(1)}, u32[]{:S(2)}, u32[]{:S(2)}) collective-permute-start(f32[1,3072]{1,0:T(1,128)S(1)} %add.23.refs_2_), channel_id=1, source_target_pairs={{0,4},{1,5},{2,6},{3,7},{4,0},{5,1},{6,2},{7,3},{8,12},{9,13},{10,... | collective-permute-start | bytes 36872 | tf_op jit(solution)/shard_map/ppermute | solution.py:373
  101.7 3.7 %collective-permute-start.24 = (f32[1,3072]{1,0:T(1,128)S(1)}, f32[1,3072]{1,0:T(1,128)S(1)}, u32[]{:S(2)}, u32[]{:S(2)}) collective-permute-start(f32[1,3072]{1,0:T(1,128)S(1)} %add.23.refs_2_), channel_id=1, source_target_pairs={{0,6},{1,7},{2,0},{3,1},{4,2},{5,3},{6,4},{7,5},{8,14},{9,15},{10,... | collective-permute-start | bytes 36872 | tf_op jit(solution)/shard_map/ppermute | solution.py:373
  107.6 11.1 %all-to-all-start.2 = ((f32[16,1,1024]{2,1,0:T(1,128)}), f32[16,1,1024]{2,1,0:T(1,128)S(1)}, u32[]{:S(2)}, u32[]{:S(2)}) async-start(f32[16,1,1024]{2,1,0:T(1,128)} %columns.3), calls=%async_computation.2 | async-start | bytes 131072 | tf_op jit(solution)/shard_map/all_to_all | solution.py:382
  (3 other events, 22.6 us)
